TPU v7x, 256 devices: a whole 4x4x8 slice. The times are simulated.
256 devices in a mesh: mp: 16 (over x_hi, z), dp: 16 (over x_lo, y, core).
Axes of the slice: x: 4 (x_hi: 2, x_lo: 2; x = x_hi * 2 + x_lo), y: 4, z: 8, core: 2. Of those that a mesh axis runs over, the one named last changes fastest.
Arguments:
- pre_act: bfloat16 [2048, 36864], P('dp', 'mp'), may hold values from -5 to 5
- cotangent: bfloat16 [2048, 10240], P('mp', 'dp'), may hold values from -6 to 6
- down_weight: bfloat16 [36864, 10240], P('mp', 'dp'), may hold values from -0.03125 to 0.03125
- first_moment: bfloat16 [36864, 10240], P('mp', 'dp'), may hold values from -8.125 to 8.125
- second_moment: bfloat16 [36864, 10240], P('mp', 'dp'), may hold values from 4.09375 to 204
Outputs:
- input_grad: bfloat16 [2048, 36864], P('dp', 'mp')
- step_update: bfloat16 [36864, 10240], P('mp', 'dp')
All inputs are finite; a program needn't handle non-finite values.
Results may differ from a plain program's by a relative error of at most 0.023.
Values may be sent and summed in bfloat16 or wider, within the bound.
No kernel may reach another device: no remote copies, remote signals or barrier semaphores. Data moves between devices by JAX's collectives and lax.ppermute only.
A program may use at most 128 MiB of HBM per device.

v0:
```python
import jax
import jax.numpy as jnp
from jax import lax
from jax.sharding import PartitionSpec as P

STEP = 20


gelu_scale = 0.7978845608028654
gelu_cubic = 0.044715
beta_one = 0.9
beta_two = 0.95
epsilon = 1e-08


def gelu_parts(values):
    tangent = jnp.tanh(gelu_scale * (values + gelu_cubic * values * values * values))
    output = 0.5 * values * (1.0 + tangent)
    slopes = 0.5 * (1.0 + tangent) + 0.5 * values * (1.0 - tangent * tangent) * gelu_scale * (
        1.0 + 3.0 * gelu_cubic * values * values
    )
    return (output, slopes)


def adam_update(gradient, first_moment, second_moment):
    moment_one = beta_one * first_moment.astype(jnp.float32) + (1.0 - beta_one) * gradient
    moment_two = (
        beta_two * second_moment.astype(jnp.float32) + (1.0 - beta_two) * gradient * gradient
    )
    corrected = moment_one / (1.0 - beta_one**STEP)
    scaled = jnp.sqrt(moment_two / (1.0 - beta_two**STEP))
    return (corrected / (scaled + epsilon)).astype(jnp.bfloat16)


def shards(pre_act, cotangent, down_weight, first_moment, second_moment):
    contract_rows = (((0,), (0,)), ((), ()))
    contract_cols = (((1,), (1,)), ((), ()))
    cot_whole = lax.all_gather(cotangent, "mp", axis=0, tiled=True)
    pre_whole = lax.all_gather(pre_act, "dp", axis=0, tiled=True)
    output, unused = gelu_parts(pre_whole.astype(jnp.float32))
    gradient = lax.dot_general(
        output.astype(jnp.bfloat16), cot_whole, contract_rows, preferred_element_type=jnp.float32
    )
    step_update = adam_update(gradient, first_moment, second_moment)
    hidden_grad = lax.psum_scatter(
        lax.dot_general(
            cot_whole, down_weight, contract_cols, preferred_element_type=jnp.float32
        ).astype(jnp.bfloat16),
        "dp",
        scatter_dimension=0,
        tiled=True,
    ).astype(jnp.float32)
    unused, slopes = gelu_parts(pre_act.astype(jnp.float32))
    input_grad = (hidden_grad * slopes).astype(jnp.bfloat16)
    return (input_grad, step_update)


def solution(mesh):
    placed = (P("dp", "mp"), P("mp", "dp"), P("mp", "dp"), P("mp", "dp"), P("mp", "dp"))
    return jax.shard_map(
        shards,
        mesh=mesh,
        in_specs=placed,
        out_specs=(P("dp", "mp"), P("mp", "dp")),
        check_vma=False,
    )
```

profile of v0, /device:TPU:96, one launch (start us, length us, event | category | flops | bytes accessed | tf_op | source)
XLA Modules:
  0.0 252.2 jit_solution(13566705437147897671)
XLA Ops:
  7.2 0.0 copy-start
  7.2 0.0 all-gather.3.cloned.1.call-start
  7.2 0.7 all-gather.3.cloned.1.call-update
  7.9 0.0 all-gather.5.cloned.1.call-start
  8.0 0.7 all-gather.5.cloned.1.call-update
  8.7 0.0 reduce-scatter.2.cloned.1.call-start
  8.7 92.5 %all-gather.3.cloned.1.call-done = bf16[2048,640]{1,0:T(8,128)(2,1)} async-done(((bf16[128,640]{1,0:T(8,128)(2,1)}), bf16[2048,640]{1,0:T(8,128)(2,1)}) %all-gather.3.cloned.1.call-update) | async-done | bytes 2621456 | tf_op jit(solution)/shard_map/all_gather | solution.py:38
  101.2 0.0 copy-done
  101.2 11.5 %convolution_convert_fusion = bf16[2048,2304]{1,0:T(8,128)(2,1)} fusion(bf16[2048,640]{1,0:T(8,128)(2,1)} %all-gather.3.cloned.1.call-done, bf16[2304,640]{1,0:T(8,128)(2,1)S(1)} %copy-done), kind=kOutput, calls=%fused_computation.10 | convolution fusion | flops 6044516352 | bytes 15007744 | tf_op jit(solution)/shard_map/dot_general | solution.py:46
  112.7 0.0 reduce-scatter.2.cloned.1.call-update
  112.7 0.0 copy-start.1
  112.7 47.5 %all-gather.5.cloned.1.call-done = bf16[2048,2304]{1,0:T(8,128)(2,1)} async-done(((bf16[128,2304]{1,0:T(8,128)(2,1)}), bf16[2048,2304]{1,0:T(8,128)(2,1)}) %all-gather.5.cloned.1.call-update) | async-done | bytes 9437200 | tf_op jit(solution)/shard_map/all_gather | solution.py:39
  160.2 19.4 %fusion.12 = bf16[2304,640]{1,0:T(8,128)(2,1)} fusion(bf16[2304,640]{1,0:T(8,128)(2,1)} %param.9, bf16[2304,640]{1,0:T(8,128)(2,1)} %param.8, bf16[2048,640]{1,0:T(8,128)(2,1)} %all-gather.3.cloned.1.call-done, bf16[2048,2304]{1,0:T(8,128)(2,1)} %all-gather.5.cloned.1.call-done), kind=kOutput, calls=%fused_computation.18 | convolution fusion | flops 6107627520 | bytes 20905984 | tf_op jit(solution)/shard_map/dot_general | solution.py:41
  179.5 63.5 %reduce-scatter.2.cloned.1.call-done = bf16[128,2304]{1,0:T(8,128)(2,1)} async-done(((bf16[2048,2304]{1,0:T(8,128)(2,1)}), bf16[128,2304]{1,0:T(8,128)(2,1)}) %reduce-scatter.2.cloned.1.call-update) | async-done | bytes 589840 | tf_op jit(solution)/shard_map/reduce_scatter | solution.py:45
  243.0 0.0 copy-done.1
  243.0 2.7 %fusion.22 = bf16[128,2304]{1,0:T(8,128)(2,1)} fusion(bf16[128,2304]{1,0:T(8,128)(2,1)S(1)} %copy-done.1, bf16[128,2304]{1,0:T(8,128)(2,1)} %reduce-scatter.2.cloned.1.call-done), kind=kLoop, calls=%fused_computation.33 | loop fusion | flops 6193152 | bytes 1769472 | tf_op jit(solution)/shard_map/convert_element_type | solution.py:54
Async XLA Ops:
  7.2 94.0 %copy-start = (bf16[2304,640]{1,0:T(8,128)(2,1)S(1)}, bf16[2304,640]{1,0:T(8,128)(2,1)}, u32[]{:S(2)}) copy-start(bf16[2304,640]{1,0:T(8,128)(2,1)} %param.7) | copy-start | bytes 8847364
  7.2 94.0 %all-gather.3.cloned.1.call-start = ((), (), s32[]{:S(2)}) async-start(), calls=%async_computation.1 | async-start | bytes 2785280 | tf_op jit(solution)/shard_map/all_gather | solution.py:38
  7.9 152.2 %all-gather.5.cloned.1.call-start = ((), (), s32[]{:S(2)}) async-start(), calls=%async_computation.3 | async-start | bytes 10027008 | tf_op jit(solution)/shard_map/all_gather | solution.py:39
  8.7 234.3 %reduce-scatter.2.cloned.1.call-start = ((), (), s32[]{:S(2)}) async-start(), calls=%async_computation.2 | async-start | bytes 10027008 | tf_op jit(solution)/shard_map/reduce_scatter | solution.py:45
  112.7 130.3 %copy-start.1 = (bf16[128,2304]{1,0:T(8,128)(2,1)S(1)}, bf16[128,2304]{1,0:T(8,128)(2,1)}, u32[]{:S(2)}) copy-start(bf16[128,2304]{1,0:T(8,128)(2,1)} %param.5) | copy-start | bytes 1769476
Sparse Core Ops, SparseCore 0:
  10.6 90.5 all-gather.2
  103.0 57.1 all-gather.4
  162.7 80.2 reduce-scatter.1
where the time goes:
time: 253 us; the launch traced here: 252 us
  waiting for transfers between devices  205 us (81%)
  matrix products  30.9 us (12%)
  between operations  13.8 us (5%)
  other arithmetic  2.7 us (1%)
    all_gather x1, waiting for transfers between devices, shards(): cot_whole = lax.all_gather(cotangent, 'mp', axis=0, tiled=True)  92.5 us
    reduce_scatter x1, waiting for transfers between devices, shards(): lax.psum_scatter(lax.dot_general(cot_whole, down_weight, contract_cols, p...  63.5 us
    all_gather x1, waiting for transfers between devices, shards(): pre_whole = lax.all_gather(pre_act, 'dp', axis=0, tiled=True)  47.5 us
    dot_general x1, matrix products, shards(): lax.dot_general(output.astype(jnp.bfloat16), cot_whole, contract_rows, pr...  19.4 us
    dot_general x1, matrix products, shards(): lax.dot_general(cot_whole, down_weight, contract_cols, preferred_element_...  11.5 us
  transfers between devices with their start and end apart: 3, of which 3 were waited for; matrix products, arithmetic and copies ran while one was open for 12% of the time, Pallas kernels for 0%

commit v1 on v0

v1 whole, which is shorter than its diff:
```python
import jax
import jax.numpy as jnp
from jax import lax
from jax.sharding import PartitionSpec as P

STEP = 20

gelu_scale = 0.7978845608028654
gelu_cubic = 0.044715
beta_one = 0.9
beta_two = 0.95
epsilon = 1e-08

f32 = jnp.float32
bf16 = jnp.bfloat16


def gelu_parts(values):
    tangent = jnp.tanh(gelu_scale * (values + gelu_cubic * values * values * values))
    output = 0.5 * values * (1.0 + tangent)
    slopes = 0.5 * (1.0 + tangent) + 0.5 * values * (1.0 - tangent * tangent) * gelu_scale * (
        1.0 + 3.0 * gelu_cubic * values * values
    )
    return (output, slopes)


def adam_update(gradient, first_moment, second_moment):
    moment_one = beta_one * first_moment.astype(f32) + (1.0 - beta_one) * gradient
    moment_two = beta_two * second_moment.astype(f32) + (1.0 - beta_two) * gradient * gradient
    corrected = moment_one / (1.0 - beta_one**STEP)
    scaled = jnp.sqrt(moment_two / (1.0 - beta_two**STEP))
    return (corrected / (scaled + epsilon)).astype(bf16)


def move_dp(x, dx, dy, dc):
    pairs = [
        (i, ((i // 8 + dx) % 2) * 8 + ((i // 2 + dy) % 4) * 2 + (i + dc) % 2) for i in range(16)
    ]
    return lax.ppermute(x, "dp", pairs)


def move_mp(x, dx, dz):
    pairs = [(i, ((i // 8 + dx) % 2) * 8 + (i + dz) % 8) for i in range(16)]
    return lax.ppermute(x, "mp", pairs)


def third(x, i):
    size = x.shape[1] // 3
    return x[:, i * size : (i + 1) * size]


def gather_mp(block):
    both = jnp.stack([block, move_mp(block, 1, 0)])
    up, down = [both], [both]
    for _ in range(3):
        up.append(move_mp(up[-1], 0, 1))
        down.append(move_mp(down[-1], 0, -1))
    far = jnp.concatenate([move_mp(up[-1][:1], 0, 1), move_mp(down[-1][1:], 0, -1)])
    parts = [both, down[1], down[2], down[3], far, up[3], up[2], up[1]]
    return jnp.stack(parts, axis=1).reshape(16, *block.shape)


ORDER = ((1, 2), (1, 1), (1, 3), (0, 2), (0, 1), (0, 3), (1, 0), (0, 0))


def gather_dp(block):
    y_prev = move_dp(block, 0, 1, 0)
    y_next = move_dp(block, 0, -1, 0)
    x_other = move_dp(block, 1, 0, 0)
    xy_next = move_dp(y_next, 1, 0, 0)
    xy_prev = move_dp(x_other, 0, 1, 0)
    y_far = move_dp(y_next, 0, -1, 0)
    xy_far = jnp.concatenate(
        [
            move_dp(third(xy_next, 0), 0, -1, 0),
            move_dp(third(xy_prev, 1), 0, 1, 0),
            move_dp(third(y_far, 2), 1, 0, 0),
        ],
        axis=1,
    )
    return jnp.concatenate([xy_far, xy_next, xy_prev, y_far, y_next, y_prev, x_other, block], axis=0)


def add(*terms):
    return sum(t.astype(f32) for t in terms).astype(bf16)


def add_third(x, i, got):
    return jnp.concatenate(
        [add(third(x, k), got) if k == i else third(x, k) for k in range(3)], axis=1
    )


def shards(pre_act, cotangent, down_weight, first_moment, second_moment):
    rows, units = pre_act.shape
    core = lax.axis_index("dp") % 2
    y = (lax.axis_index("dp") // 2) % 4
    x_lo = lax.axis_index("dp") // 8
    x_hi = lax.axis_index("mp") // 8
    z = lax.axis_index("mp") % 8
    contract_rows = (((0,), (0,)), ((), ()))
    contract_cols = (((1,), (1,)), ((), ()))

    hidden = gelu_parts(pre_act.astype(f32))[0].astype(bf16)
    weight = jnp.concatenate([down_weight, move_dp(down_weight, 0, 0, 1)], axis=1)

    cot = gather_mp(cotangent)

    def place(dx, dy, parity):
        z_of = ((y + dy) % 4) * 2 + parity
        return ((x_lo + dx - x_hi) % 2) * 8 + (z_of - z) % 8

    def pick(parity):
        return jnp.concatenate(
            [lax.dynamic_index_in_dim(cot, place(dx, dy, parity), 0, False) for dx, dy in ORDER],
            axis=0,
        )

    cot_own = pick(core)
    cot_give = pick(1 - core)
    cot_got = move_dp(cot_give, 0, 0, 1)
    cot_wide = jnp.concatenate([cot_own, cot_got], axis=1)

    def partial(lo, hi):
        return lax.optimization_barrier(
            lax.dot_general(
                cot_wide[lo * rows : hi * rows], weight, contract_cols, preferred_element_type=f32
            ).astype(bf16)
        )

    hid = gather_dp(hidden)
    hid, cot_wide = lax.optimization_barrier((hid, cot_wide))

    xy_far = partial(0, 1)
    got0 = move_dp(third(xy_far, 0), 0, 1, 0)
    got1 = move_dp(third(xy_far, 1), 0, -1, 0)
    got2 = move_dp(third(xy_far, 2), 1, 0, 0)
    mid = partial(1, 4)
    near = partial(4, 8)
    xy_next, xy_prev, y_far = mid[:rows], mid[rows : 2 * rows], mid[2 * rows :]
    y_next, y_prev, x_other, mine = (near[k * rows : (k + 1) * rows] for k in range(4))
    got0, got1, got2 = lax.optimization_barrier((got0, got1, got2))
    got_x = move_dp(add_third(xy_next, 0, got0), 1, 0, 0)
    got_m = move_dp(add_third(xy_prev, 1, got1), 0, -1, 0)
    got_y = move_dp(add_third(y_far, 2, got2), 0, 1, 0)
    got_x, got_m, got_y = lax.optimization_barrier((got_x, got_m, got_y))
    end_prev = move_dp(y_prev, 0, -1, 0)
    end_next = move_dp(add(y_next, got_x, got_y), 0, 1, 0)
    end_x = move_dp(add(x_other, got_m), 1, 0, 0)

    hid_other = move_dp(hid, 0, 0, 1)
    gradient = lax.dot_general(hid, cot_own, contract_rows, preferred_element_type=f32)
    gradient += lax.dot_general(hid_other, cot_give, contract_rows, preferred_element_type=f32)
    step_update = adam_update(gradient, first_moment, second_moment)

    hidden_grad = sum(t.astype(f32) for t in (mine, end_prev, end_next, end_x))
    slopes = gelu_parts(pre_act.astype(f32))[1]
    return ((hidden_grad * slopes).astype(bf16), step_update)


def solution(mesh):
    placed = (P("dp", "mp"), P("mp", "dp"), P("mp", "dp"), P("mp", "dp"), P("mp", "dp"))
    return jax.shard_map(
        shards,
        mesh=mesh,
        in_specs=placed,
        out_specs=(P("dp", "mp"), P("mp", "dp")),
        check_vma=False,
    )
```

time: 253 us -> 132 us (0.52)
  waiting for transfers between devices: 205 us -> 50 us
  starting transfers between devices: 0.11 us -> 41.4 us
  between operations: 13.8 us -> 1.07 us
  local copies, waits for them, and re-layouts: 0.02 us -> 7.21 us
  matrix products: 30.9 us -> 24.4 us
  other arithmetic: 2.7 us -> 5.67 us
    all_gather x2 -> x0, waiting for transfers between devices: 140 us -> none  [the longest x1 92.5 us: shards(): cot_whole = lax.all_gather(cotangent, 'mp', axis=0, tiled=True)]
    reduce_scatter x1 -> x0, waiting for transfers between devices: 63.5 us -> none  [shards(): lax.psum_scatter(lax.dot_general(cot_whole, down_weight, contract_cols, p...]
    ppermute x0 -> x30, waiting for transfers between devices: none -> 50 us  [the longest x21 39.1 us: move_dp(): return lax.ppermute(x, 'dp', pairs)]
    ppermute x0 -> x30, starting transfers between devices: none -> 41.4 us  [the longest x21 25.1 us: move_dp(): return lax.ppermute(x, 'dp', pairs)]
    dot_general x2 -> x5, matrix products: 30.9 us -> 24.4 us  [the longest x1 10.7 us: shards(): lax.dot_general(hid_other, cot_give, contract_rows, preferred_element_typ...]
    unnamed x4 -> x33, local copies, waits for them, and re-layouts: 0.02 us -> 6.38 us
  transfers between devices with their start and end apart: 3 -> 30, of which waited for: 3 -> 15; matrix products, arithmetic and copies ran while one was open for 12% -> 18% of each run, Pallas kernels for 0% -> 0%
where the time goes in v1:
time: 132 us; the launch traced here: 130 us
  waiting for transfers between devices  50 us (38%)
  starting transfers between devices  41.4 us (31%)
  matrix products  24.4 us (18%)
  local copies, waits for them, and re-layouts  7.21 us (5%)
  other arithmetic  5.67 us (4%)
    ppermute x21, waiting for transfers between devices, move_dp(): return lax.ppermute(x, 'dp', pairs)  39.1 us
    ppermute x21, starting transfers between devices, move_dp(): return lax.ppermute(x, 'dp', pairs)  25.1 us
    ppermute x9, starting transfers between devices, move_mp(): return lax.ppermute(x, 'mp', pairs)  16.3 us
    ppermute x9, waiting for transfers between devices, move_mp(): return lax.ppermute(x, 'mp', pairs)  11 us
    dot_general x1, matrix products, shards(): lax.dot_general(hid_other, cot_give, contract_rows, preferred_element_typ...  10.7 us
    dot_general x3, matrix products, partial(): lax.dot_general(cot_wide[lo * rows:hi * rows], weight, contract_cols, pre...  7.99 us
    unnamed x33, local copies, waits for them, and re-layouts  6.38 us
    dot_general x1, matrix products, shards(): lax.dot_general(hid, cot_own, contract_rows, preferred_element_type=f32)  5.79 us
  transfers between devices with their start and end apart: 30, of which 15 were waited for; matrix products, arithmetic and copies ran while one was open for 18% of the time, Pallas kernels for 0%

profile of v1, /device:TPU:96, one launch (start us, length us, event | category | flops | bytes accessed | tf_op | source)
XLA Modules:
  0.0 129.8 jit_solution(1796198193601568418)
XLA Ops:
  0.6 3.1 %collective-permute-start.9 = (bf16[128,640]{1,0:T(8,128)(2,1)}, bf16[128,640]{1,0:T(8,128)(2,1)S(1)}, u32[]{:S(2)}, u32[]{:S(2)}) collective-permute-start(bf16[128,640]{1,0:T(8,128)(2,1)} %param.6), channel_id=1, source_target_pairs={{0,128},{16,144},{32,160},{48,176},{64,192},{80,208},{96,224},{112... | collective-permute-start | bytes 491528 | tf_op jit(solution)/shard_map/ppermute | solution.py:44
  3.7 4.6 %collective-permute-done.9 = bf16[128,640]{1,0:T(8,128)(2,1)S(1)} collective-permute-done((bf16[128,640]{1,0:T(8,128)(2,1)}, bf16[128,640]{1,0:T(8,128)(2,1)S(1)}, u32[]{:S(2)}, u32[]{:S(2)}) %collective-permute-start.9) | collective-permute-done | bytes 163872 | tf_op jit(solution)/shard_map/ppermute | solution.py:44
  9.5 3.1 %collective-permute-start.13 = (bf16[2,128,640]{2,1,0:T(8,128)(2,1)S(1)}, bf16[2,128,640]{2,1,0:T(8,128)(2,1)S(1)}, u32[]{:S(2)}, u32[]{:S(2)}) collective-permute-start(bf16[2,128,640]{2,1,0:T(8,128)(2,1)S(1)} %pad_maximum_fusion.4), channel_id=1, source_target_pairs={{0,16},{16,32},{32,48},{48,64},{64,80},{80,96},{96,112},{112,0},{1... | collective-permute-start | bytes 983048 | tf_op jit(solution)/shard_map/ppermute | solution.py:44
  14.1 3.1 %collective-permute-start = (bf16[128,2304]{1,0:T(8,128)(2,1)S(1)}, bf16[128,2304]{1,0:T(8,128)(2,1)S(1)}, u32[]{:S(2)}, u32[]{:S(2)}) collective-permute-start(bf16[128,2304]{1,0:T(8,128)(2,1)S(1)} %fusion.9), channel_id=1, source_target_pairs={{0,6},{1,7},{2,0},{3,1},{4,2},{5,3},{6,4},{7,5},{8,14},{9,15},{10,... | collective-permute-start | bytes 1769480 | tf_op jit(solution)/shard_map/ppermute | solution.py:39
  19.4 3.2 %collective-permute-start.14 = (bf16[2,128,640]{2,1,0:T(8,128)(2,1)S(1)}, bf16[2,128,640]{2,1,0:T(8,128)(2,1)S(1)}, u32[]{:S(2)}, u32[]{:S(2)}) collective-permute-start(bf16[2,128,640]{2,1,0:T(8,128)(2,1)S(1)} %collective-permute-done.13), channel_id=1, source_target_pairs={{0,16},{16,32},{32,48},{48,64},{64,80},{80,96},{96,112},{112,0},{1... | collective-permute-start | bytes 983048 | tf_op jit(solution)/shard_map/ppermute | solution.py:44
  22.6 3.7 %constant_dynamic-update-slice_fusion.8 = bf16[2304,1280]{1,0:T(8,128)(2,1)} fusion(bf16[2304,640]{1,0:T(8,128)(2,1)} %param.7), kind=kLoop, calls=%fused_computation.75 | loop fusion | bytes 5898240
  26.4 2.3 %collective-permute-done = bf16[128,2304]{1,0:T(8,128)(2,1)S(1)} collective-permute-done((bf16[128,2304]{1,0:T(8,128)(2,1)S(1)}, bf16[128,2304]{1,0:T(8,128)(2,1)S(1)}, u32[]{:S(2)}, u32[]{:S(2)}) %collective-permute-start) | collective-permute-done | bytes 589856 | tf_op jit(solution)/shard_map/ppermute | solution.py:39
  28.6 3.7 %collective-permute-start.6 = (bf16[128,2304]{1,0:T(8,128)(2,1)S(1)}, bf16[128,2304]{1,0:T(8,128)(2,1)S(1)}, u32[]{:S(2)}, u32[]{:S(2)}) collective-permute-start(bf16[128,2304]{1,0:T(8,128)(2,1)S(1)} %collective-permute-done), channel_id=1, source_target_pairs={{0,6},{1,7},{2,0},{3,1},{4,2},{5,3},{6,4},{7,5},{8,14},{9,15},{10,... | collective-permute-start | bytes 1769480 | tf_op jit(solution)/shard_map/ppermute | solution.py:39
  33.9 3.2 %collective-permute-start.15 = (bf16[2,128,640]{2,1,0:T(8,128)(2,1)S(1)}, bf16[2,128,640]{2,1,0:T(8,128)(2,1)S(1)}, u32[]{:S(2)}, u32[]{:S(2)}) collective-permute-start(bf16[2,128,640]{2,1,0:T(8,128)(2,1)S(1)} %collective-permute-done.14), channel_id=1, source_target_pairs={{0,16},{16,32},{32,48},{48,64},{64,80},{80,96},{96,112},{112,0},{1... | collective-permute-start | bytes 983048 | tf_op jit(solution)/shard_map/ppermute | solution.py:44
  37.2 5.0 %collective-permute-done.12 = bf16[2,128,640]{2,1,0:T(8,128)(2,1)S(1)} collective-permute-done((bf16[2,128,640]{2,1,0:T(8,128)(2,1)S(1)}, bf16[2,128,640]{2,1,0:T(8,128)(2,1)S(1)}, u32[]{:S(2)}, u32[]{:S(2)}) %collective-permute-start.12) | collective-permute-done | bytes 327712 | tf_op jit(solution)/shard_map/ppermute | solution.py:44
  42.3 3.3 %collective-permute-start.16 = (bf16[1,128,640]{2,1,0:T(8,128)(2,1)S(1)}, bf16[1,128,640]{2,1,0:T(8,128)(2,1)S(1)}, u32[]{:S(2)}, u32[]{:S(2)}) collective-permute-start(bf16[1,128,640]{2,1,0:T(8,128)(2,1)S(1)} %slice.107), channel_id=1, source_target_pairs={{0,16},{16,32},{32,48},{48,64},{64,80},{80,96},{96,112},{112,0},{1... | collective-permute-start | bytes 491528 | tf_op jit(solution)/shard_map/ppermute | solution.py:44
  48.8 3.2 %collective-permute-start.2 = (bf16[128,768]{1,0:T(8,128)(2,1)S(1)}, bf16[128,768]{1,0:T(8,128)(2,1)S(1)}, u32[]{:S(2)}, u32[]{:S(2)}) collective-permute-start(bf16[128,768]{1,0:T(8,128)(2,1)S(1)} %slice.104), channel_id=1, source_target_pairs={{0,6},{1,7},{2,0},{3,1},{4,2},{5,3},{6,4},{7,5},{8,14},{9,15},{10,... | collective-permute-start | bytes 589832 | tf_op jit(solution)/shard_map/ppermute | solution.py:39
  53.5 14.0 %collective-permute-done.5 = bf16[128,768]{1,0:T(8,128)(2,1)S(1)} collective-permute-done((bf16[128,768]{1,0:T(8,128)(2,1)S(1)}, bf16[128,768]{1,0:T(8,128)(2,1)S(1)}, u32[]{:S(2)}, u32[]{:S(2)}) %collective-permute-start.5) | collective-permute-done | bytes 196640 | tf_op jit(solution)/shard_map/ppermute | solution.py:39
  71.0 2.5 %convolution_convert_fusion.1 = bf16[384,2304]{1,0:T(8,128)(2,1)S(1)} fusion(bf16[2304,1280]{1,0:T(8,128)(2,1)S(1)} %constant_dynamic-update-slice_fusion.7, bf16[1024,1280]{1,0:T(8,128)(2,1)S(1)} %pad_maximum_fusion), kind=kOutput, calls=%fused_computation.8 | convolution fusion | flops 2265808896 | bytes 8650752 | tf_op jit(solution)/shard_map/dot_general | solution.py:126
  75.7 3.2 %collective-permute-start.22 = (bf16[128,768]{1,0:T(8,128)(2,1)S(1)}, bf16[128,768]{1,0:T(8,128)(2,1)S(1)}, u32[]{:S(2)}, u32[]{:S(2)}) collective-permute-start(bf16[128,768]{1,0:T(8,128)(2,1)S(1)} %get-tuple-element.44), channel_id=1, source_target_pairs={{0,6},{1,7},{2,0},{3,1},{4,2},{5,3},{6,4},{7,5},{8,14},{9,15},{10,... | collective-permute-start | bytes 589832 | tf_op jit(solution)/shard_map/ppermute | solution.py:39
  79.5 3.9 %collective-permute-done.21 = bf16[128,768]{1,0:T(8,128)(2,1)S(1)} collective-permute-done((bf16[128,768]{1,0:T(8,128)(2,1)S(1)}, bf16[128,768]{1,0:T(8,128)(2,1)S(1)}, u32[]{:S(2)}, u32[]{:S(2)}) %collective-permute-start.21) | collective-permute-done | bytes 196640 | tf_op jit(solution)/shard_map/ppermute | solution.py:39
  88.2 3.5 %convolution_convert_fusion = bf16[512,2304]{1,0:T(8,128)(2,1)S(1)} fusion(bf16[2304,1280]{1,0:T(8,128)(2,1)S(1)} %constant_dynamic-update-slice_fusion.7, bf16[1024,1280]{1,0:T(8,128)(2,1)S(1)} %pad_maximum_fusion), kind=kOutput, calls=%fused_computation.7 | convolution fusion | flops 3021078528 | bytes 9568256 | tf_op jit(solution)/shard_map/dot_general | solution.py:126
  91.8 2.8 %collective-permute-start.20 = (bf16[128,2304]{1,0:T(8,128)(2,1)S(1)}, bf16[128,2304]{1,0:T(8,128)(2,1)S(1)}, u32[]{:S(2)}, u32[]{:S(2)}) collective-permute-start(bf16[128,2304]{1,0:T(8,128)(2,1)S(1)} %slice.110), channel_id=1, source_target_pairs={{0,6},{1,7},{2,0},{3,1},{4,2},{5,3},{6,4},{7,5},{8,14},{9,15},{10,... | collective-permute-start | bytes 1769480 | tf_op jit(solution)/shard_map/ppermute | solution.py:39
  94.6 4.1 %collective-permute-done.24 = bf16[128,2304]{1,0:T(8,128)(2,1)S(1)} collective-permute-done((bf16[128,2304]{1,0:T(8,128)(2,1)S(1)}, bf16[128,2304]{1,0:T(8,128)(2,1)S(1)}, u32[]{:S(2)}, u32[]{:S(2)}) %collective-permute-start.24) | collective-permute-done | bytes 589856 | tf_op jit(solution)/shard_map/ppermute | solution.py:39
  98.7 3.7 %collective-permute-done.25 = bf16[128,2304]{1,0:T(8,128)(2,1)S(1)} collective-permute-done((bf16[128,2304]{1,0:T(8,128)(2,1)S(1)}, bf16[128,2304]{1,0:T(8,128)(2,1)S(1)}, u32[]{:S(2)}, u32[]{:S(2)}) %collective-permute-start.25) | collective-permute-done | bytes 589856 | tf_op jit(solution)/shard_map/ppermute | solution.py:39
  104.3 5.8 %fusion.24 = f32[2304,640]{1,0:T(8,128)} fusion(bf16[1024,2304]{1,0:T(8,128)(2,1)S(1)} %constant_dynamic-update-slice_fusion, bf16[1024,640]{1,0:T(8,128)(2,1)S(1)} %get-tuple-element.18), kind=kOutput, calls=%fused_computation.79 | convolution fusion | flops 3019898880 | bytes 11927552 | tf_op jit(solution)/shard_map/dot_general | solution.py:152
  111.9 2.9 %collective-permute-done.28 = bf16[128,2304]{1,0:T(8,128)(2,1)S(1)} collective-permute-done((bf16[128,2304]{1,0:T(8,128)(2,1)S(1)}, bf16[128,2304]{1,0:T(8,128)(2,1)S(1)}, u32[]{:S(2)}, u32[]{:S(2)}) %collective-permute-start.28) | collective-permute-done | bytes 589856 | tf_op jit(solution)/shard_map/ppermute | solution.py:39
  114.9 2.4 %collective-permute-done.27 = bf16[128,2304]{1,0:T(8,128)(2,1)S(1)} collective-permute-done((bf16[128,2304]{1,0:T(8,128)(2,1)S(1)}, bf16[128,2304]{1,0:T(8,128)(2,1)S(1)}, u32[]{:S(2)}, u32[]{:S(2)}) %collective-permute-start.27) | collective-permute-done | bytes 589856 | tf_op jit(solution)/shard_map/ppermute | solution.py:39
  119.2 10.7 %fusion.5 = bf16[2304,640]{1,0:T(8,128)(2,1)} fusion(bf16[2304,640]{1,0:T(8,128)(2,1)S(1)} %copy-done.3, f32[2304,640]{1,0:T(8,128)} %fusion.24, bf16[2304,640]{1,0:T(8,128)(2,1)S(1)} %copy-done.4, bf16[1024,2304]{1,0:T(8,128)(2,1)S(1)} %collective-permute-done.29, bf16[1024,640]{1,0:T(8,128)(2,1)S(1)} %get-tuple-element.19), kind=kOutput, calls=%fused_computation.6 | convolution fusion | flops 3042017280 | bytes 20774912 | tf_op jit(solution)/shard_map/dot_general | solution.py:153
  (100 shorter events, 27.7 us)
Async XLA Ops:
  9.3 10.0 %collective-permute-start.10 = (bf16[2,128,640]{2,1,0:T(8,128)(2,1)S(1)}, bf16[2,128,640]{2,1,0:T(8,128)(2,1)S(1)}, u32[]{:S(2)}, u32[]{:S(2)}) collective-permute-start(bf16[2,128,640]{2,1,0:T(8,128)(2,1)S(1)} %pad_maximum_fusion.4), channel_id=1, source_target_pairs={{0,112},{16,0},{32,16},{48,32},{64,48},{80,64},{96,80},{112,96},{1... | collective-permute-start | bytes 983048 | tf_op jit(solution)/shard_map/ppermute | solution.py:44
  9.5 9.9 %collective-permute-start.13 = (bf16[2,128,640]{2,1,0:T(8,128)(2,1)S(1)}, bf16[2,128,640]{2,1,0:T(8,128)(2,1)S(1)}, u32[]{:S(2)}, u32[]{:S(2)}) collective-permute-start(bf16[2,128,640]{2,1,0:T(8,128)(2,1)S(1)} %pad_maximum_fusion.4), channel_id=1, source_target_pairs={{0,16},{16,32},{32,48},{48,64},{64,80},{80,96},{96,112},{112,0},{1... | collective-permute-start | bytes 983048 | tf_op jit(solution)/shard_map/ppermute | solution.py:44
  14.1 14.5 %collective-permute-start = (bf16[128,2304]{1,0:T(8,128)(2,1)S(1)}, bf16[128,2304]{1,0:T(8,128)(2,1)S(1)}, u32[]{:S(2)}, u32[]{:S(2)}) collective-permute-start(bf16[128,2304]{1,0:T(8,128)(2,1)S(1)} %fusion.9), channel_id=1, source_target_pairs={{0,6},{1,7},{2,0},{3,1},{4,2},{5,3},{6,4},{7,5},{8,14},{9,15},{10,... | collective-permute-start | bytes 1769480 | tf_op jit(solution)/shard_map/ppermute | solution.py:39
  17.2 16.6 %collective-permute-start.3 = (bf16[128,2304]{1,0:T(8,128)(2,1)S(1)}, bf16[128,2304]{1,0:T(8,128)(2,1)S(1)}, u32[]{:S(2)}, u32[]{:S(2)}) collective-permute-start(bf16[128,2304]{1,0:T(8,128)(2,1)S(1)} %fusion.9), channel_id=1, source_target_pairs={{0,8},{1,9},{2,10},{3,11},{4,12},{5,13},{6,14},{7,15},{8,0},{9,1},... | collective-permute-start | bytes 1769480 | tf_op jit(solution)/shard_map/ppermute | solution.py:39
  19.4 14.5 %collective-permute-start.11 = (bf16[2,128,640]{2,1,0:T(8,128)(2,1)S(1)}, bf16[2,128,640]{2,1,0:T(8,128)(2,1)S(1)}, u32[]{:S(2)}, u32[]{:S(2)}) collective-permute-start(bf16[2,128,640]{2,1,0:T(8,128)(2,1)S(1)} %collective-permute-done.10), channel_id=1, source_target_pairs={{0,112},{16,0},{32,16},{48,32},{64,48},{80,64},{96,80},{112,96},{1... | collective-permute-start | bytes 983048 | tf_op jit(solution)/shard_map/ppermute | solution.py:44
  19.4 14.5 %collective-permute-start.14 = (bf16[2,128,640]{2,1,0:T(8,128)(2,1)S(1)}, bf16[2,128,640]{2,1,0:T(8,128)(2,1)S(1)}, u32[]{:S(2)}, u32[]{:S(2)}) collective-permute-start(bf16[2,128,640]{2,1,0:T(8,128)(2,1)S(1)} %collective-permute-done.13), channel_id=1, source_target_pairs={{0,16},{16,32},{32,48},{48,64},{64,80},{80,96},{96,112},{112,0},{1... | collective-permute-start | bytes 983048 | tf_op jit(solution)/shard_map/ppermute | solution.py:44
  28.6 17.0 %collective-permute-start.6 = (bf16[128,2304]{1,0:T(8,128)(2,1)S(1)}, bf16[128,2304]{1,0:T(8,128)(2,1)S(1)}, u32[]{:S(2)}, u32[]{:S(2)}) collective-permute-start(bf16[128,2304]{1,0:T(8,128)(2,1)S(1)} %collective-permute-done), channel_id=1, source_target_pairs={{0,6},{1,7},{2,0},{3,1},{4,2},{5,3},{6,4},{7,5},{8,14},{9,15},{10,... | collective-permute-start | bytes 1769480 | tf_op jit(solution)/shard_map/ppermute | solution.py:39
  32.3 15.1 %collective-permute-start.1 = (bf16[128,2304]{1,0:T(8,128)(2,1)S(1)}, bf16[128,2304]{1,0:T(8,128)(2,1)S(1)}, u32[]{:S(2)}, u32[]{:S(2)}) collective-permute-start(bf16[128,2304]{1,0:T(8,128)(2,1)S(1)} %collective-permute-done), channel_id=1, source_target_pairs={{0,8},{1,9},{2,10},{3,11},{4,12},{5,13},{6,14},{7,15},{8,0},{9,1},... | collective-permute-start | bytes 1769480 | tf_op jit(solution)/shard_map/ppermute | solution.py:39
  33.8 13.6 %collective-permute-start.4 = (bf16[128,2304]{1,0:T(8,128)(2,1)S(1)}, bf16[128,2304]{1,0:T(8,128)(2,1)S(1)}, u32[]{:S(2)}, u32[]{:S(2)}) collective-permute-start(bf16[128,2304]{1,0:T(8,128)(2,1)S(1)} %collective-permute-done.3), channel_id=1, source_target_pairs={{0,2},{1,3},{2,4},{3,5},{4,6},{5,7},{6,0},{7,1},{8,10},{9,11},{10,... | collective-permute-start | bytes 1769480 | tf_op jit(solution)/shard_map/ppermute | solution.py:39
  33.8 8.4 %collective-permute-start.12 = (bf16[2,128,640]{2,1,0:T(8,128)(2,1)S(1)}, bf16[2,128,640]{2,1,0:T(8,128)(2,1)S(1)}, u32[]{:S(2)}, u32[]{:S(2)}) collective-permute-start(bf16[2,128,640]{2,1,0:T(8,128)(2,1)S(1)} %collective-permute-done.11), channel_id=1, source_target_pairs={{0,112},{16,0},{32,16},{48,32},{64,48},{80,64},{96,80},{112,96},{1... | collective-permute-start | bytes 983048 | tf_op jit(solution)/shard_map/ppermute | solution.py:44
  33.9 8.4 %collective-permute-start.15 = (bf16[2,128,640]{2,1,0:T(8,128)(2,1)S(1)}, bf16[2,128,640]{2,1,0:T(8,128)(2,1)S(1)}, u32[]{:S(2)}, u32[]{:S(2)}) collective-permute-start(bf16[2,128,640]{2,1,0:T(8,128)(2,1)S(1)} %collective-permute-done.14), channel_id=1, source_target_pairs={{0,16},{16,32},{32,48},{48,64},{64,80},{80,96},{96,112},{112,0},{1... | collective-permute-start | bytes 983048 | tf_op jit(solution)/shard_map/ppermute | solution.py:44
  45.7 24.0 %collective-permute-start.19 = (bf16[2304,640]{1,0:T(8,128)(2,1)S(1)}, bf16[2304,640]{1,0:T(8,128)(2,1)S(1)}, u32[]{:S(2)}, u32[]{:S(2)}) collective-permute-start(bf16[2304,640]{1,0:T(8,128)(2,1)S(1)} %copy-done.1), channel_id=1, source_target_pairs={{0,1},{1,0},{2,3},{3,2},{4,5},{5,4},{6,7},{7,6},{8,9},{9,8},{10,11... | collective-permute-start | bytes 8847368 | tf_op jit(solution)/shard_map/ppermute | solution.py:39
  47.4 20.3 %collective-permute-start.8 = (bf16[128,2304]{1,0:T(8,128)(2,1)S(1)}, bf16[128,2304]{1,0:T(8,128)(2,1)S(1)}, u32[]{:S(2)}, u32[]{:S(2)}) collective-permute-start(bf16[128,2304]{1,0:T(8,128)(2,1)S(1)} %fusion.9), channel_id=1, source_target_pairs={{0,2},{1,3},{2,4},{3,5},{4,6},{5,7},{6,0},{7,1},{8,10},{9,11},{10,... | collective-permute-start | bytes 1769480 | tf_op jit(solution)/shard_map/ppermute | solution.py:39
  48.8 18.7 %collective-permute-start.5 = (bf16[128,768]{1,0:T(8,128)(2,1)S(1)}, bf16[128,768]{1,0:T(8,128)(2,1)S(1)}, u32[]{:S(2)}, u32[]{:S(2)}) collective-permute-start(bf16[128,768]{1,0:T(8,128)(2,1)S(1)} %slice.105), channel_id=1, source_target_pairs={{0,2},{1,3},{2,4},{3,5},{4,6},{5,7},{6,0},{7,1},{8,10},{9,11},{10,... | collective-permute-start | bytes 589832 | tf_op jit(solution)/shard_map/ppermute | solution.py:39
  48.8 18.7 %collective-permute-start.2 = (bf16[128,768]{1,0:T(8,128)(2,1)S(1)}, bf16[128,768]{1,0:T(8,128)(2,1)S(1)}, u32[]{:S(2)}, u32[]{:S(2)}) collective-permute-start(bf16[128,768]{1,0:T(8,128)(2,1)S(1)} %slice.104), channel_id=1, source_target_pairs={{0,6},{1,7},{2,0},{3,1},{4,2},{5,3},{6,4},{7,5},{8,14},{9,15},{10,... | collective-permute-start | bytes 589832 | tf_op jit(solution)/shard_map/ppermute | solution.py:39
  53.5 15.9 %collective-permute-start.18 = (bf16[1024,640]{1,0:T(8,128)(2,1)S(1)}, bf16[1024,640]{1,0:T(8,128)(2,1)S(1)}, u32[]{:S(2)}, u32[]{:S(2)}) collective-permute-start(bf16[1024,640]{1,0:T(8,128)(2,1)S(1)} %get-tuple-element.19), channel_id=1, source_target_pairs={{0,1},{1,0},{2,3},{3,2},{4,5},{5,4},{6,7},{7,6},{8,9},{9,8},{10,11... | collective-permute-start | bytes 3932168 | tf_op jit(solution)/shard_map/ppermute | solution.py:39
  69.6 49.6 %collective-permute-start.29 = (bf16[1024,2304]{1,0:T(8,128)(2,1)S(1)}, bf16[1024,2304]{1,0:T(8,128)(2,1)S(1)}, u32[]{:S(2)}, u32[]{:S(2)}) collective-permute-start(bf16[1024,2304]{1,0:T(8,128)(2,1)S(1)} %constant_dynamic-update-slice_fusion), channel_id=1, source_target_pairs={{0,1},{1,0},{2,3},{3,2},{4,5},{5,4},{6,7},{7,6},{8,9},{9,8},{10,11... | collective-permute-start | bytes 14155784 | tf_op jit(solution)/shard_map/ppermute | solution.py:39
  75.6 7.8 %collective-permute-start.21 = (bf16[128,768]{1,0:T(8,128)(2,1)S(1)}, bf16[128,768]{1,0:T(8,128)(2,1)S(1)}, u32[]{:S(2)}, u32[]{:S(2)}) collective-permute-start(bf16[128,768]{1,0:T(8,128)(2,1)S(1)} %get-tuple-element.45), channel_id=1, source_target_pairs={{0,2},{1,3},{2,4},{3,5},{4,6},{5,7},{6,0},{7,1},{8,10},{9,11},{10,... | collective-permute-start | bytes 589832 | tf_op jit(solution)/shard_map/ppermute | solution.py:39
  85.1 13.6 %collective-permute-start.24 = (bf16[128,2304]{1,0:T(8,128)(2,1)S(1)}, bf16[128,2304]{1,0:T(8,128)(2,1)S(1)}, u32[]{:S(2)}, u32[]{:S(2)}) collective-permute-start(bf16[128,2304]{1,0:T(8,128)(2,1)S(1)} %pad_maximum_fusion.1), channel_id=1, source_target_pairs={{0,8},{1,9},{2,10},{3,11},{4,12},{5,13},{6,14},{7,15},{8,0},{9,1},... | collective-permute-start | bytes 1769480 | tf_op jit(solution)/shard_map/ppermute | solution.py:39
  85.8 16.6 %collective-permute-start.25 = (bf16[128,2304]{1,0:T(8,128)(2,1)S(1)}, bf16[128,2304]{1,0:T(8,128)(2,1)S(1)}, u32[]{:S(2)}, u32[]{:S(2)}) collective-permute-start(bf16[128,2304]{1,0:T(8,128)(2,1)S(1)} %pad_maximum_fusion.2), channel_id=1, source_target_pairs={{0,6},{1,7},{2,0},{3,1},{4,2},{5,3},{6,4},{7,5},{8,14},{9,15},{10,... | collective-permute-start | bytes 1769480 | tf_op jit(solution)/shard_map/ppermute | solution.py:39
  87.6 14.7 %collective-permute-start.26 = (bf16[128,2304]{1,0:T(8,128)(2,1)S(1)}, bf16[128,2304]{1,0:T(8,128)(2,1)S(1)}, u32[]{:S(2)}, u32[]{:S(2)}) collective-permute-start(bf16[128,2304]{1,0:T(8,128)(2,1)S(1)} %pad_maximum_fusion.3), channel_id=1, source_target_pairs={{0,2},{1,3},{2,4},{3,5},{4,6},{5,7},{6,0},{7,1},{8,10},{9,11},{10,... | collective-permute-start | bytes 1769480 | tf_op jit(solution)/shard_map/ppermute | solution.py:39
  91.8 20.2 %collective-permute-start.20 = (bf16[128,2304]{1,0:T(8,128)(2,1)S(1)}, bf16[128,2304]{1,0:T(8,128)(2,1)S(1)}, u32[]{:S(2)}, u32[]{:S(2)}) collective-permute-start(bf16[128,2304]{1,0:T(8,128)(2,1)S(1)} %slice.110), channel_id=1, source_target_pairs={{0,6},{1,7},{2,0},{3,1},{4,2},{5,3},{6,4},{7,5},{8,14},{9,15},{10,... | collective-permute-start | bytes 1769480 | tf_op jit(solution)/shard_map/ppermute | solution.py:39
  102.7 12.1 %collective-permute-start.28 = (bf16[128,2304]{1,0:T(8,128)(2,1)S(1)}, bf16[128,2304]{1,0:T(8,128)(2,1)S(1)}, u32[]{:S(2)}, u32[]{:S(2)}) collective-permute-start(bf16[128,2304]{1,0:T(8,128)(2,1)S(1)} %get-tuple-element.35), channel_id=1, source_target_pairs={{0,8},{1,9},{2,10},{3,11},{4,12},{5,13},{6,14},{7,15},{8,0},{9,1},... | collective-permute-start | bytes 1769480 | tf_op jit(solution)/shard_map/ppermute | solution.py:39
  104.3 13.0 %collective-permute-start.27 = (bf16[128,2304]{1,0:T(8,128)(2,1)S(1)}, bf16[128,2304]{1,0:T(8,128)(2,1)S(1)}, u32[]{:S(2)}, u32[]{:S(2)}) collective-permute-start(bf16[128,2304]{1,0:T(8,128)(2,1)S(1)} %get-tuple-element.34), channel_id=1, source_target_pairs={{0,2},{1,3},{2,4},{3,5},{4,6},{5,7},{6,0},{7,1},{8,10},{9,11},{10,... | collective-permute-start | bytes 1769480 | tf_op jit(solution)/shard_map/ppermute | solution.py:39
  (13 other events, 102.3 us)

commit v2 on v0

v2 whole, which is shorter than its diff:
```python
import functools

import jax
import jax.numpy as jnp
from jax import lax
from jax.experimental import pallas as pl
from jax.experimental.pallas import tpu as pltpu
from jax.sharding import PartitionSpec as P

STEP = 20

gelu_scale = 0.7978845608028654
gelu_cubic = 0.044715
beta_one = 0.9
beta_two = 0.95
epsilon = 1e-08

f32 = jnp.float32
bf16 = jnp.bfloat16
barrier = lax.optimization_barrier
VMEM = 40 << 20


def gelu_parts(values):
    tangent = jnp.tanh(gelu_scale * (values + gelu_cubic * values * values * values))
    output = 0.5 * values * (1.0 + tangent)
    slopes = 0.5 * (1.0 + tangent) + 0.5 * values * (1.0 - tangent * tangent) * gelu_scale * (
        1.0 + 3.0 * gelu_cubic * values * values
    )
    return (output, slopes)


def adam_update(gradient, first_moment, second_moment):
    scale_one = 1.0 / (1.0 - beta_one**STEP)
    scale_two = 1.0 / (1.0 - beta_two**STEP)
    corrected = (beta_one * scale_one) * first_moment.astype(f32)
    corrected += ((1.0 - beta_one) * scale_one) * gradient
    scaled = (beta_two * scale_two) * second_moment.astype(f32)
    scaled += ((1.0 - beta_two) * scale_two) * (gradient * gradient)
    return (corrected / (jnp.sqrt(scaled) + epsilon)).astype(bf16)


def move_dp(x, dx, dy, dc):
    pairs = [
        (i, ((i // 8 + dx) % 2) * 8 + ((i // 2 + dy) % 4) * 2 + (i + dc) % 2) for i in range(16)
    ]
    return lax.ppermute(x, "dp", pairs)


def move_mp(x, dx, dz):
    pairs = [(i, ((i // 8 + dx) % 2) * 8 + (i + dz) % 8) for i in range(16)]
    return lax.ppermute(x, "mp", pairs)


ORDER = ((1, 2), (1, 1), (1, 3), (0, 2), (0, 1), (0, 3), (1, 0), (0, 0))


def turn_kernel(pre_act, hidden):
    hidden[...] = gelu_parts(pre_act[...].astype(f32))[0].T.astype(bf16)


def slope_kernel(pre_act, slopes):
    slopes[...] = gelu_parts(pre_act[...].astype(f32))[1]


def local(kernel, pre_act, turn, dtype, cost, tile=768):
    rows, units = pre_act.shape
    across = pl.BlockSpec((rows, tile), lambda j: (0, j))
    along = pl.BlockSpec((tile, rows), lambda j: (j, 0))
    return pl.pallas_call(
        kernel,
        grid=(units // tile,),
        in_specs=[across],
        out_specs=along if turn else across,
        out_shape=jax.ShapeDtypeStruct((units, rows) if turn else (rows, units), dtype),
        cost_estimate=pl.CostEstimate(
            flops=20 * rows * units, bytes_accessed=cost, transcendentals=rows * units
        ),
    )(pre_act)


def gradient_kernel(thirds, per, *refs):
    pieces, (cot, own, other, first) = refs[thirds:-4], refs[-4:]
    width = first.shape[1]
    for n in range(thirds):

        @pl.when(pl.program_id(0) // per == n)
        def _(n=n):
            first[...] = refs[n][...]

    hidden = jnp.concatenate([first[...], *(ref[...] for ref in pieces)], axis=1)
    half = own.shape[1]
    gradient = jnp.dot(hidden, cot[...], preferred_element_type=f32)
    own[...] = gradient[:, :half]
    other[...] = gradient[:, half:].astype(bf16)


def gradients(thirds, pieces, cot, tile):
    units, rows = pieces[0].shape
    tokens, features = cot.shape
    per = thirds[0].shape[0] // tile
    specs = [
        pl.BlockSpec((tile, rows), lambda j, n=n: (jnp.clip(j - n * per, 0, per - 1), 0))
        for n in range(len(thirds))
    ]
    specs += [pl.BlockSpec((tile, rows), lambda j: (j, 0))] * len(pieces)
    specs += [pl.BlockSpec((tokens, features), lambda j: (0, 0))]
    out = pl.BlockSpec((tile, features // 2), lambda j: (j, 0))
    return pl.pallas_call(
        functools.partial(gradient_kernel, len(thirds), per),
        grid=(units // tile,),
        in_specs=specs,
        out_specs=[out, out],
        out_shape=[
            jax.ShapeDtypeStruct((units, features // 2), f32),
            jax.ShapeDtypeStruct((units, features // 2), bf16),
        ],
        scratch_shapes=[pltpu.VMEM((tile, rows), bf16)],
        compiler_params=pltpu.CompilerParams(vmem_limit_bytes=VMEM),
        cost_estimate=pl.CostEstimate(
            flops=2 * tokens * units * features, bytes_accessed=18 << 20, transcendentals=0
        ),
    )(*thirds, *pieces, cot)


def adam_kernel(own, got, first, second, out):
    out[...] = adam_update(own[...] + got[...].astype(f32), first[...], second[...])


def adam(own, got, first_moment, second_moment, tile):
    units, features = own.shape
    block = pl.BlockSpec((tile, features), lambda j: (j, 0))
    return pl.pallas_call(
        adam_kernel,
        grid=(units // tile,),
        in_specs=[block] * 4,
        out_specs=block,
        out_shape=jax.ShapeDtypeStruct((units, features), bf16),
        compiler_params=pltpu.CompilerParams(vmem_limit_bytes=24 << 20),
        cost_estimate=pl.CostEstimate(
            flops=0, bytes_accessed=12 * units * features, transcendentals=0
        ),
    )(own, got, first_moment, second_moment)


def places(dp, mp):
    block = jnp.arange(16, dtype=jnp.int32)
    z = (mp + block) % 8
    code = ((mp // 8 + block // 8 + dp // 8) % 2) * 4 + (z // 2 - dp // 2) % 4
    slot = sum(jnp.where(code == dx * 4 + dy, i, 0) for i, (dx, dy) in enumerate(ORDER))
    return (slot + 8 * ((z + dp) % 2)).astype(jnp.int32)


def collect_kernel(plan, where, *refs):
    pieces, (own, give) = refs[:-2], refs[-2:]
    depth = pieces[0].shape[1]
    for piece, part, block in plan:
        row = pl.multiple_of(where[block] % 8 * depth, depth)

        @pl.when(where[block] < 8)
        def _():
            own[pl.ds(row, depth)] = pieces[piece][part]

        @pl.when(where[block] >= 8)
        def _():
            give[pl.ds(row, depth)] = pieces[piece][part]


def collect(where, pieces, plan):
    depth, width = pieces[0].shape[1:]
    whole = lambda shape: pl.BlockSpec(shape, lambda j, w: (0,) * len(shape))
    shape = (8 * depth, width)
    return pl.pallas_call(
        functools.partial(collect_kernel, plan),
        out_shape=[jax.ShapeDtypeStruct(shape, bf16)] * 2,
        grid_spec=pltpu.PrefetchScalarGridSpec(
            num_scalar_prefetch=1,
            grid=(1,),
            in_specs=[whole(p.shape) for p in pieces],
            out_specs=[whole(shape)] * 2,
        ),
        compiler_params=pltpu.CompilerParams(vmem_limit_bytes=16 << 20),
        cost_estimate=pl.CostEstimate(
            flops=0, bytes_accessed=60 * depth * width, transcendentals=0
        ),
    )(where, *pieces)


def swap(x):
    return move_dp(x, 0, 0, 1)


def add(*terms):
    return sum(t.astype(f32) for t in terms).astype(bf16)


def add_third(x, i, got):
    size = got.shape[1]
    return add(x, jnp.pad(got, ((0, 0), (i * size, (2 - i) * size))))


def shards(pre_act, cotangent, down_weight, first_moment, second_moment):
    rows, units = pre_act.shape
    features = cotangent.shape[1]
    dp = lax.axis_index("dp")
    mp = lax.axis_index("mp")
    contract_cols = (((1,), (1,)), ((), ()))

    partner = move_mp(cotangent, 1, 0)
    weight = move_dp(down_weight, 0, 0, 1)
    hidden = local(turn_kernel, pre_act, True, bf16, 32 << 20)
    where = places(dp, mp)
    partner, where, _ = barrier((partner, where, hidden))

    both = jnp.stack([cotangent, partner])
    up, down = [both], [both]
    weight = jnp.concatenate([down_weight, weight], axis=1)
    slopes = local(slope_kernel, pre_act, False, f32, 16 << 20)
    for n in range(3):
        up.append(move_mp(up[-1], 0, 1))
        down.append(move_mp(down[-1], 0, -1))
        if n == 0:
            up[1], down[1], weight, slopes = barrier((up[1], down[1], weight, slopes))
    x_other = move_dp(hidden, 1, 0, 0)
    y_prev = move_dp(hidden, 0, 1, 0)
    y_next = move_dp(hidden, 0, -1, 0)
    x_other, y_prev = barrier((x_other, y_prev))
    xy_next = move_dp(y_next, 1, 0, 0)
    xy_prev = move_dp(x_other, 0, 1, 0)
    y_far = move_dp(y_next, 0, -1, 0)
    up[3], down[3], xy_next, xy_prev, y_far = barrier(
        (up[3], down[3], xy_next, xy_prev, y_far)
    )
    size = units // 3
    cut = lambda x, i: x[i * size : (i + 1) * size]
    xy_far = [
        move_dp(cut(xy_next, 0), 0, -1, 0),
        move_dp(cut(xy_prev, 1), 0, 1, 0),
        move_dp(cut(y_far, 2), 1, 0, 0),
    ]
    pieces = [both, *down[1:], *up[1:], move_mp(up[3][:1], 0, 1), move_mp(down[3][1:], 0, -1)]
    plan = [(n, f, 8 * f + (n if n < 4 else 11 - n)) for n in range(7) for f in range(2)]
    plan += [(7, 0, 4), (8, 0, 12)]
    cot_own, cot_give = collect(where, barrier(pieces), plan)
    cot_wide = jnp.concatenate([cot_own, swap(cot_give)], axis=1)

    def partial(lo, hi):
        return barrier(
            lax.dot_general(
                cot_wide[lo * rows : hi * rows], weight, contract_cols, preferred_element_type=f32
            ).astype(bf16)
        )

    split = lambda x: [x[k * rows : (k + 1) * rows] for k in range(4)]
    third = lambda x, i: x[:, i * size : (i + 1) * size]
    p_far, p_xy_next, p_xy_prev, p_y_far = split(partial(0, 4))
    got0 = move_dp(third(p_far, 0), 0, 1, 0)
    got1 = move_dp(third(p_far, 1), 0, -1, 0)
    got2 = move_dp(third(p_far, 2), 1, 0, 0)
    near = partial(4, 8)
    got0, got1, got2, near, cot_wide, xy_far = barrier(
        (got0, got1, got2, near, cot_wide, xy_far)
    )
    p_next, p_prev, p_x, p_mine = split(near)
    got_x = move_dp(add_third(p_xy_next, 0, got0), 1, 0, 0)
    got_m = move_dp(add_third(p_xy_prev, 1, got1), 0, -1, 0)
    got_y = move_dp(add_third(p_y_far, 2, got2), 0, 1, 0)
    sent = [xy_next, xy_prev, y_far, y_next, y_prev, x_other, hidden]
    grad_own, grad_give = gradients(xy_far, sent, cot_wide, units // 3)
    got_x, got_m, got_y, grad_own, grad_give, p_prev = barrier(
        (got_x, got_m, got_y, grad_own, grad_give, p_prev)
    )
    p_next, p_x, grad_give = barrier((add(p_next, got_x, got_y), add(p_x, got_m), grad_give))
    end_next = move_dp(p_next, 0, 1, 0)
    end_x = move_dp(p_x, 1, 0, 0)
    end_prev = move_dp(p_prev, 0, -1, 0)
    step_update = adam(grad_own, swap(grad_give), first_moment, second_moment, units // 6)
    end_prev, end_next, end_x, step_update = barrier((end_prev, end_next, end_x, step_update))

    hidden_grad = sum(t.astype(f32) for t in (p_mine, end_prev, end_next, end_x))
    return ((hidden_grad * slopes).astype(bf16), step_update)


def solution(mesh):
    placed = (P("dp", "mp"), P("mp", "dp"), P("mp", "dp"), P("mp", "dp"), P("mp", "dp"))
    return jax.shard_map(
        shards,
        mesh=mesh,
        in_specs=placed,
        out_specs=(P("dp", "mp"), P("mp", "dp")),
        check_vma=False,
    )
```

time: 253 us -> 109 us (0.43)
  waiting for transfers between devices: 205 us -> 36 us
  starting transfers between devices: 0.11 us -> 36.3 us
  matrix products: 30.9 us -> 7.01 us
  Pallas kernels: 0 us -> 20.4 us
  between operations: 13.8 us -> 0.88 us
  local copies, waits for them, and re-layouts: 0.02 us -> 3.19 us
    all_gather x2 -> x0, waiting for transfers between devices: 140 us -> none  [the longest x1 92.5 us: shards(): cot_whole = lax.all_gather(cotangent, 'mp', axis=0, tiled=True)]
    reduce_scatter x1 -> x0, waiting for transfers between devices: 63.5 us -> none  [shards(): lax.psum_scatter(lax.dot_general(cot_whole, down_weight, contract_cols, p...]
    ppermute x0 -> x30, starting transfers between devices: none -> 36.3 us  [the longest x21 23.5 us: move_dp(): return lax.ppermute(x, 'dp', pairs)]
    ppermute x0 -> x30, waiting for transfers between devices: none -> 36 us  [the longest x21 21.5 us: move_dp(): return lax.ppermute(x, 'dp', pairs)]
    dot_general x2, matrix products: 30.9 us -> 7.01 us  [partial(): lax.dot_general(cot_wide[lo * rows:hi * rows], weight, contract_cols, pre...]
    pallas_call x0 -> x5, Pallas kernels: none -> 20.4 us  [the longest x1 7.94 us: gradients(): pl.pallas_call(functools.partial(gradient_kernel, len(thirds), per), grid...]
    concatenate x0 -> x1, other arithmetic: none -> 3.16 us  [shards(): weight = jnp.concatenate([down_weight, weight], axis=1)]
    unnamed x4 -> x13, local copies, waits for them, and re-layouts: 0.02 us -> 2.81 us
  transfers between devices with their start and end apart: 3 -> 30, of which waited for: 3 -> 16; matrix products, arithmetic and copies ran while one was open for 12% -> 10% of each run, Pallas kernels for 0% -> 18%
where the time goes in v2:
time: 109 us
  starting transfers between devices  36.3 us (33%)
  waiting for transfers between devices  36 us (33%)
  Pallas kernels  20.4 us (19%)
  matrix products  7.01 us (6%)
  other arithmetic  4.87 us (4%)
  local copies, waits for them, and re-layouts  3.19 us (3%)
    ppermute x21, starting transfers between devices, move_dp(): return lax.ppermute(x, 'dp', pairs)  23.5 us
    ppermute x21, waiting for transfers between devices, move_dp(): return lax.ppermute(x, 'dp', pairs)  21.5 us
    ppermute x9, waiting for transfers between devices, move_mp(): return lax.ppermute(x, 'mp', pairs)  14.5 us
    ppermute x9, starting transfers between devices, move_mp(): return lax.ppermute(x, 'mp', pairs)  12.7 us
    pallas_call x1, Pallas kernels, gradients(): pl.pallas_call(functools.partial(gradient_kernel, len(thirds), per), grid...  7.94 us
    dot_general x2, matrix products, partial(): lax.dot_general(cot_wide[lo * rows:hi * rows], weight, contract_cols, pre...  7.01 us
    pallas_call x2, Pallas kernels, local(): pl.pallas_call(kernel, grid=(units // tile,), in_specs=[across], out_spec...  6.34 us
    pallas_call x1, Pallas kernels, adam(): pl.pallas_call(adam_kernel, grid=(units // tile,), in_specs=[block] * 4,...  5.12 us
  transfers between devices with their start and end apart: 30, of which 16 were waited for; matrix products, arithmetic and copies ran while one was open for 10% of the time, Pallas kernels for 18%

profile of v2, /device:TPU:96, one launch (start us, length us, event | category | flops | bytes accessed | tf_op | source)
XLA Modules:
  0.0 108.6 jit_solution(13123578840220103292)
XLA Ops:
  0.7 3.1 %collective-permute-start = (bf16[128,640]{1,0:T(8,128)(2,1)}, bf16[128,640]{1,0:T(8,128)(2,1)S(1)}, u32[]{:S(2)}, u32[]{:S(2)}) collective-permute-start(bf16[128,640]{1,0:T(8,128)(2,1)} %param.6), channel_id=1, source_target_pairs={{0,128},{16,144},{32,160},{48,176},{64,192},{80,208},{96,224},{112... | collective-permute-start | bytes 491528 | tf_op jit(solution)/shard_map/ppermute | solution.py:52
  3.9 3.0 %shard_map.68.refs_9_ = bf16[2304,128]{1,0:T(8,128)(2,1)} custom-call(bf16[128,2304]{1,0:T(8,128)(2,1)} %pre_act.3), custom_call_target="tpu_custom_call" | custom-call | flops 5898240 | bytes 33554432 | tf_op jit(solution)/shard_map/pallas_call | solution.py:70
  6.9 3.0 %collective-permute-start.8 = (bf16[2304,128]{1,0:T(8,128)(2,1)}, bf16[2304,128]{1,0:T(8,128)(2,1)S(1)}, u32[]{:S(2)}, u32[]{:S(2)}) collective-permute-start(bf16[2304,128]{1,0:T(8,128)(2,1)} %shard_map.68.refs_9_), channel_id=1, source_target_pairs={{0,6},{1,7},{2,0},{3,1},{4,2},{5,3},{6,4},{7,5},{8,14},{9,15},{10,... | collective-permute-start | bytes 1769480 | tf_op jit(solution)/shard_map/ppermute | solution.py:47
  10.5 3.3 %shard_map.69 = f32[128,2304]{1,0:T(8,128)} custom-call(bf16[128,2304]{1,0:T(8,128)(2,1)} %pre_act.3), custom_call_target="tpu_custom_call" | custom-call | flops 5898240 | bytes 16777216 | tf_op jit(solution)/shard_map/pallas_call | solution.py:70
  13.9 3.2 %collective-permute-start.1 = (bf16[2,128,640]{2,1,0:T(8,128)(2,1)S(1)}, bf16[2,128,640]{2,1,0:T(8,128)(2,1)S(1)}, u32[]{:S(2)}, u32[]{:S(2)}) collective-permute-start(bf16[2,128,640]{2,1,0:T(8,128)(2,1)S(1)} %pad_maximum_fusion.1.refs_0_), channel_id=1, source_target_pairs={{0,16},{16,32},{32,48},{48,64},{64,80},{80,96},{96,112},{112,0},{1... | collective-permute-start | bytes 983048 | tf_op jit(solution)/shard_map/ppermute | solution.py:52
  17.1 3.2 %pad_maximum_fusion = bf16[2304,1280]{1,0:T(8,128)(2,1)S(1)} fusion(bf16[2304,640]{1,0:T(8,128)(2,1)} %collective-permute-done.3, bf16[2304,640]{1,0:T(8,128)(2,1)} %param.7), kind=kLoop, calls=%fused_computation | loop fusion | flops 11796480 | bytes 11796480 | tf_op jit(solution)/shard_map/concatenate | solution.py:217
  20.3 3.6 %collective-permute-done.1.refs_4_ = bf16[2,128,640]{2,1,0:T(8,128)(2,1)S(1)} collective-permute-done((bf16[2,128,640]{2,1,0:T(8,128)(2,1)S(1)}, bf16[2,128,640]{2,1,0:T(8,128)(2,1)S(1)}, u32[]{:S(2)}, u32[]{:S(2)}) %collective-permute-start.1) | collective-permute-done | bytes 327712 | tf_op jit(solution)/shard_map/ppermute | solution.py:52
  23.8 3.4 %collective-permute-done.2.refs_1_ = bf16[2,128,640]{2,1,0:T(8,128)(2,1)S(1)} collective-permute-done((bf16[2,128,640]{2,1,0:T(8,128)(2,1)S(1)}, bf16[2,128,640]{2,1,0:T(8,128)(2,1)S(1)}, u32[]{:S(2)}, u32[]{:S(2)}) %collective-permute-start.2) | collective-permute-done | bytes 327712 | tf_op jit(solution)/shard_map/ppermute | solution.py:52
  31.1 2.9 %collective-permute-start.13 = (bf16[2304,128]{1,0:T(8,128)(2,1)S(1)}, bf16[2304,128]{1,0:T(8,128)(2,1)S(1)}, u32[]{:S(2)}, u32[]{:S(2)}) collective-permute-start(bf16[2304,128]{1,0:T(8,128)(2,1)S(1)} %collective-permute-done.8.refs_6_), channel_id=1, source_target_pairs={{0,6},{1,7},{2,0},{3,1},{4,2},{5,3},{6,4},{7,5},{8,14},{9,15},{10,... | collective-permute-start | bytes 1769480 | tf_op jit(solution)/shard_map/ppermute | solution.py:47
  37.3 5.2 %collective-permute-done.9.refs_3_ = bf16[2304,128]{1,0:T(8,128)(2,1)S(1)} collective-permute-done((bf16[2304,128]{1,0:T(8,128)(2,1)S(1)}, bf16[2304,128]{1,0:T(8,128)(2,1)S(1)}, u32[]{:S(2)}, u32[]{:S(2)}) %collective-permute-start.9) | collective-permute-done | bytes 589856 | tf_op jit(solution)/shard_map/ppermute | solution.py:47
  42.4 2.4 %collective-permute-done.12.refs_4_ = bf16[2304,128]{1,0:T(8,128)(2,1)S(1)} collective-permute-done((bf16[2304,128]{1,0:T(8,128)(2,1)S(1)}, bf16[2304,128]{1,0:T(8,128)(2,1)S(1)}, u32[]{:S(2)}, u32[]{:S(2)}) %collective-permute-start.12) | collective-permute-done | bytes 589856 | tf_op jit(solution)/shard_map/ppermute | solution.py:47
  47.7 3.0 %collective-permute-done.14.refs_7_ = bf16[1,128,640]{2,1,0:T(8,128)(2,1)S(1)} collective-permute-done((bf16[1,128,640]{2,1,0:T(8,128)(2,1)S(1)}, bf16[1,128,640]{2,1,0:T(8,128)(2,1)S(1)}, u32[]{:S(2)}, u32[]{:S(2)}) %collective-permute-start.14) | collective-permute-done | bytes 163872 | tf_op jit(solution)/shard_map/ppermute | solution.py:52
  50.8 2.7 %collective-permute-done.15.refs_8_ = bf16[1,128,640]{2,1,0:T(8,128)(2,1)S(1)} collective-permute-done((bf16[1,128,640]{2,1,0:T(8,128)(2,1)S(1)}, bf16[1,128,640]{2,1,0:T(8,128)(2,1)S(1)}, u32[]{:S(2)}, u32[]{:S(2)}) %collective-permute-start.15) | collective-permute-done | bytes 163872 | tf_op jit(solution)/shard_map/ppermute | solution.py:52
  54.6 3.0 %collective-permute-start.20 = (bf16[768,128]{1,0:T(8,128)(2,1)S(1)}, bf16[768,128]{1,0:T(8,128)(2,1)S(1)}, u32[]{:S(2)}, u32[]{:S(2)}) collective-permute-start(bf16[768,128]{1,0:T(8,128)(2,1)S(1)} %slice.62), channel_id=1, source_target_pairs={{0,6},{1,7},{2,0},{3,1},{4,2},{5,3},{6,4},{7,5},{8,14},{9,15},{10,... | collective-permute-start | bytes 589832 | tf_op jit(solution)/shard_map/ppermute | solution.py:47
  58.8 3.5 %convolution_convert_fusion.1 = bf16[512,2304]{1,0:T(8,128)(2,1)S(1)} fusion(bf16[2304,1280]{1,0:T(8,128)(2,1)S(1)} %pad_maximum_fusion, bf16[1024,1280]{1,0:T(8,128)(2,1)S(1)} %constant_dynamic-update-slice_fusion.refs_10_), kind=kOutput, calls=%fused_computation.2 | convolution fusion | flops 3021078528 | bytes 9568256 | tf_op jit(solution)/shard_map/dot_general | solution.py:249
  62.5 3.3 %collective-permute-start.18 = (bf16[128,768]{1,0:T(8,128)(2,1)S(1)}, bf16[128,768]{1,0:T(8,128)(2,1)S(1)}, u32[]{:S(2)}, u32[]{:S(2)}) collective-permute-start(bf16[128,768]{1,0:T(8,128)(2,1)S(1)} %get-tuple-element.102), channel_id=1, source_target_pairs={{0,6},{1,7},{2,0},{3,1},{4,2},{5,3},{6,4},{7,5},{8,14},{9,15},{10,... | collective-permute-start | bytes 589832 | tf_op jit(solution)/shard_map/ppermute | solution.py:47
  67.3 3.5 %convolution_convert_fusion = bf16[512,2304]{1,0:T(8,128)(2,1)S(1)} fusion(bf16[2304,1280]{1,0:T(8,128)(2,1)S(1)} %pad_maximum_fusion, bf16[1024,1280]{1,0:T(8,128)(2,1)S(1)} %constant_dynamic-update-slice_fusion.refs_10_), kind=kOutput, calls=%fused_computation.1 | convolution fusion | flops 3021078528 | bytes 9568256 | tf_op jit(solution)/shard_map/dot_general | solution.py:249
  75.8 7.9 %shard_map.71 = (f32[2304,640]{1,0:T(8,128)}, bf16[2304,640]{1,0:T(8,128)(2,1)S(1)}) custom-call(bf16[768,128]{1,0:T(8,128)(2,1)S(1)} %collective-permute-done.20.refs_0_, bf16[768,128]{1,0:T(8,128)(2,1)S(1)} %collective-permute-done.21.refs_1_, bf16[768,128]{1,0:T(8,128)(2,1)S(1)} %collective-permute-done.22.refs_2_, ...), custom_call_target="tpu_custom_call" | custom-call | flops 6039797760 | bytes 18874368 | tf_op jit(solution)/shard_map/pallas_call | solution.py:109
  83.7 2.2 %collective-permute-done.23 = bf16[128,2304]{1,0:T(8,128)(2,1)S(1)} collective-permute-done((bf16[128,2304]{1,0:T(8,128)(2,1)S(1)}, bf16[128,2304]{1,0:T(8,128)(2,1)S(1)}, u32[]{:S(2)}, u32[]{:S(2)}) %collective-permute-start.23) | collective-permute-done | bytes 589856 | tf_op jit(solution)/shard_map/ppermute | solution.py:47
  87.1 2.7 %collective-permute-done.25 = bf16[128,2304]{1,0:T(8,128)(2,1)S(1)} collective-permute-done((bf16[128,2304]{1,0:T(8,128)(2,1)S(1)}, bf16[128,2304]{1,0:T(8,128)(2,1)S(1)}, u32[]{:S(2)}, u32[]{:S(2)}) %collective-permute-start.25) | collective-permute-done | bytes 589856 | tf_op jit(solution)/shard_map/ppermute | solution.py:47
  92.9 2.7 %collective-permute-done.29.got = bf16[2304,640]{1,0:T(8,128)(2,1)S(1)} collective-permute-done((bf16[2304,640]{1,0:T(8,128)(2,1)S(1)}, bf16[2304,640]{1,0:T(8,128)(2,1)S(1)}, u32[]{:S(2)}, u32[]{:S(2)}) %collective-permute-start.29) | collective-permute-done | bytes 2949152 | tf_op jit(solution)/shard_map/ppermute | solution.py:47
  95.6 2.7 %copy-done = f32[2304,640]{1,0:T(8,128)S(1)} copy-done((f32[2304,640]{1,0:T(8,128)S(1)}, f32[2304,640]{1,0:T(8,128)}, u32[]{:S(2)}) %copy-start) | copy-done | bytes 5898264
  98.3 5.1 %shard_map.72 = bf16[2304,640]{1,0:T(8,128)(2,1)} custom-call(f32[2304,640]{1,0:T(8,128)S(1)} %copy-done, bf16[2304,640]{1,0:T(8,128)(2,1)S(1)} %collective-permute-done.29.got, bf16[2304,640]{1,0:T(8,128)(2,1)S(1)} %copy-done.1, bf16[2304,640]{1,0:T(8,128)(2,1)S(1)} %copy-done.2), custom_call_target="tpu_custom_call" | custom-call | bytes 17694720 | tf_op jit(solution)/shard_map/pallas_call | solution.py:133
  103.4 2.6 %collective-permute-done.26 = bf16[128,2304]{1,0:T(8,128)(2,1)S(1)} collective-permute-done((bf16[128,2304]{1,0:T(8,128)(2,1)S(1)}, bf16[128,2304]{1,0:T(8,128)(2,1)S(1)}, u32[]{:S(2)}, u32[]{:S(2)}) %collective-permute-start.26) | collective-permute-done | bytes 589856 | tf_op jit(solution)/shard_map/ppermute | solution.py:47
  (70 shorter events, 26.5 us)
Async XLA Ops:
  0.6 16.5 %collective-permute-start.3 = (bf16[2304,640]{1,0:T(8,128)(2,1)}, bf16[2304,640]{1,0:T(8,128)(2,1)}, u32[]{:S(2)}, u32[]{:S(2)}) collective-permute-start(bf16[2304,640]{1,0:T(8,128)(2,1)} %param.7), channel_id=1, source_target_pairs={{0,1},{1,0},{2,3},{3,2},{4,5},{5,4},{6,7},{7,6},{8,9},{9,8},{10,11... | collective-permute-start | bytes 8847368 | tf_op jit(solution)/shard_map/ppermute | solution.py:47
  0.7 13.1 %collective-permute-start = (bf16[128,640]{1,0:T(8,128)(2,1)}, bf16[128,640]{1,0:T(8,128)(2,1)S(1)}, u32[]{:S(2)}, u32[]{:S(2)}) collective-permute-start(bf16[128,640]{1,0:T(8,128)(2,1)} %param.6), channel_id=1, source_target_pairs={{0,128},{16,144},{32,160},{48,176},{64,192},{80,208},{96,224},{112... | collective-permute-start | bytes 491528 | tf_op jit(solution)/shard_map/ppermute | solution.py:52
  6.9 22.4 %collective-permute-start.8 = (bf16[2304,128]{1,0:T(8,128)(2,1)}, bf16[2304,128]{1,0:T(8,128)(2,1)S(1)}, u32[]{:S(2)}, u32[]{:S(2)}) collective-permute-start(bf16[2304,128]{1,0:T(8,128)(2,1)} %shard_map.68.refs_9_), channel_id=1, source_target_pairs={{0,6},{1,7},{2,0},{3,1},{4,2},{5,3},{6,4},{7,5},{8,14},{9,15},{10,... | collective-permute-start | bytes 1769480 | tf_op jit(solution)/shard_map/ppermute | solution.py:47
  9.9 19.4 %collective-permute-start.10 = (bf16[2304,128]{1,0:T(8,128)(2,1)}, bf16[2304,128]{1,0:T(8,128)(2,1)S(1)}, u32[]{:S(2)}, u32[]{:S(2)}) collective-permute-start(bf16[2304,128]{1,0:T(8,128)(2,1)} %shard_map.68.refs_9_), channel_id=1, source_target_pairs={{0,8},{1,9},{2,10},{3,11},{4,12},{5,13},{6,14},{7,15},{8,0},{9,1},... | collective-permute-start | bytes 1769480 | tf_op jit(solution)/shard_map/ppermute | solution.py:47
  10.5 18.8 %collective-permute-start.11 = (bf16[2304,128]{1,0:T(8,128)(2,1)}, bf16[2304,128]{1,0:T(8,128)(2,1)S(1)}, u32[]{:S(2)}, u32[]{:S(2)}) collective-permute-start(bf16[2304,128]{1,0:T(8,128)(2,1)} %shard_map.68.refs_9_), channel_id=1, source_target_pairs={{0,2},{1,3},{2,4},{3,5},{4,6},{5,7},{6,0},{7,1},{8,10},{9,11},{10,... | collective-permute-start | bytes 1769480 | tf_op jit(solution)/shard_map/ppermute | solution.py:47
  13.9 9.9 %collective-permute-start.1 = (bf16[2,128,640]{2,1,0:T(8,128)(2,1)S(1)}, bf16[2,128,640]{2,1,0:T(8,128)(2,1)S(1)}, u32[]{:S(2)}, u32[]{:S(2)}) collective-permute-start(bf16[2,128,640]{2,1,0:T(8,128)(2,1)S(1)} %pad_maximum_fusion.1.refs_0_), channel_id=1, source_target_pairs={{0,16},{16,32},{32,48},{48,64},{64,80},{80,96},{96,112},{112,0},{1... | collective-permute-start | bytes 983048 | tf_op jit(solution)/shard_map/ppermute | solution.py:52
  17.1 10.1 %collective-permute-start.2 = (bf16[2,128,640]{2,1,0:T(8,128)(2,1)S(1)}, bf16[2,128,640]{2,1,0:T(8,128)(2,1)S(1)}, u32[]{:S(2)}, u32[]{:S(2)}) collective-permute-start(bf16[2,128,640]{2,1,0:T(8,128)(2,1)S(1)} %pad_maximum_fusion.1.refs_0_), channel_id=1, source_target_pairs={{0,112},{16,0},{32,16},{48,32},{64,48},{80,64},{96,80},{112,96},{1... | collective-permute-start | bytes 983048 | tf_op jit(solution)/shard_map/ppermute | solution.py:52
  27.5 9.5 %collective-permute-start.4 = (bf16[2,128,640]{2,1,0:T(8,128)(2,1)S(1)}, bf16[2,128,640]{2,1,0:T(8,128)(2,1)S(1)}, u32[]{:S(2)}, u32[]{:S(2)}) collective-permute-start(bf16[2,128,640]{2,1,0:T(8,128)(2,1)S(1)} %collective-permute-done.2.refs_1_), channel_id=1, source_target_pairs={{0,112},{16,0},{32,16},{48,32},{64,48},{80,64},{96,80},{112,96},{1... | collective-permute-start | bytes 983048 | tf_op jit(solution)/shard_map/ppermute | solution.py:52
  29.3 13.1 %collective-permute-start.9 = (bf16[2304,128]{1,0:T(8,128)(2,1)S(1)}, bf16[2304,128]{1,0:T(8,128)(2,1)S(1)}, u32[]{:S(2)}, u32[]{:S(2)}) collective-permute-start(bf16[2304,128]{1,0:T(8,128)(2,1)S(1)} %collective-permute-done.8.refs_6_), channel_id=1, source_target_pairs={{0,8},{1,9},{2,10},{3,11},{4,12},{5,13},{6,14},{7,15},{8,0},{9,1},... | collective-permute-start | bytes 1769480 | tf_op jit(solution)/shard_map/ppermute | solution.py:47
  30.8 14.0 %collective-permute-start.12 = (bf16[2304,128]{1,0:T(8,128)(2,1)S(1)}, bf16[2304,128]{1,0:T(8,128)(2,1)S(1)}, u32[]{:S(2)}, u32[]{:S(2)}) collective-permute-start(bf16[2304,128]{1,0:T(8,128)(2,1)S(1)} %collective-permute-done.10.refs_8_), channel_id=1, source_target_pairs={{0,2},{1,3},{2,4},{3,5},{4,6},{5,7},{6,0},{7,1},{8,10},{9,11},{10,... | collective-permute-start | bytes 1769480 | tf_op jit(solution)/shard_map/ppermute | solution.py:47
  31.1 13.7 %collective-permute-start.13 = (bf16[2304,128]{1,0:T(8,128)(2,1)S(1)}, bf16[2304,128]{1,0:T(8,128)(2,1)S(1)}, u32[]{:S(2)}, u32[]{:S(2)}) collective-permute-start(bf16[2304,128]{1,0:T(8,128)(2,1)S(1)} %collective-permute-done.8.refs_6_), channel_id=1, source_target_pairs={{0,6},{1,7},{2,0},{3,1},{4,2},{5,3},{6,4},{7,5},{8,14},{9,15},{10,... | collective-permute-start | bytes 1769480 | tf_op jit(solution)/shard_map/ppermute | solution.py:47
  35.2 9.6 %collective-permute-start.6 = (bf16[2,128,640]{2,1,0:T(8,128)(2,1)S(1)}, bf16[2,128,640]{2,1,0:T(8,128)(2,1)S(1)}, u32[]{:S(2)}, u32[]{:S(2)}) collective-permute-start(bf16[2,128,640]{2,1,0:T(8,128)(2,1)S(1)} %collective-permute-done.5.refs_5_), channel_id=1, source_target_pairs={{0,16},{16,32},{32,48},{48,64},{64,80},{80,96},{96,112},{112,0},{1... | collective-permute-start | bytes 983048 | tf_op jit(solution)/shard_map/ppermute | solution.py:52
  37.0 8.3 %collective-permute-start.7 = (bf16[2,128,640]{2,1,0:T(8,128)(2,1)S(1)}, bf16[2,128,640]{2,1,0:T(8,128)(2,1)S(1)}, u32[]{:S(2)}, u32[]{:S(2)}) collective-permute-start(bf16[2,128,640]{2,1,0:T(8,128)(2,1)S(1)} %collective-permute-done.4.refs_2_), channel_id=1, source_target_pairs={{0,112},{16,0},{32,16},{48,32},{64,48},{80,64},{96,80},{112,96},{1... | collective-permute-start | bytes 983048 | tf_op jit(solution)/shard_map/ppermute | solution.py:52
  54.6 11.1 %collective-permute-start.20 = (bf16[768,128]{1,0:T(8,128)(2,1)S(1)}, bf16[768,128]{1,0:T(8,128)(2,1)S(1)}, u32[]{:S(2)}, u32[]{:S(2)}) collective-permute-start(bf16[768,128]{1,0:T(8,128)(2,1)S(1)} %slice.62), channel_id=1, source_target_pairs={{0,6},{1,7},{2,0},{3,1},{4,2},{5,3},{6,4},{7,5},{8,14},{9,15},{10,... | collective-permute-start | bytes 589832 | tf_op jit(solution)/shard_map/ppermute | solution.py:47
  57.7 13.1 %collective-permute-start.21 = (bf16[768,128]{1,0:T(8,128)(2,1)S(1)}, bf16[768,128]{1,0:T(8,128)(2,1)S(1)}, u32[]{:S(2)}, u32[]{:S(2)}) collective-permute-start(bf16[768,128]{1,0:T(8,128)(2,1)S(1)} %slice.63), channel_id=1, source_target_pairs={{0,2},{1,3},{2,4},{3,5},{4,6},{5,7},{6,0},{7,1},{8,10},{9,11},{10,... | collective-permute-start | bytes 589832 | tf_op jit(solution)/shard_map/ppermute | solution.py:47
  57.8 13.0 %collective-permute-start.22 = (bf16[768,128]{1,0:T(8,128)(2,1)S(1)}, bf16[768,128]{1,0:T(8,128)(2,1)S(1)}, u32[]{:S(2)}, u32[]{:S(2)}) collective-permute-start(bf16[768,128]{1,0:T(8,128)(2,1)S(1)} %slice.64), channel_id=1, source_target_pairs={{0,8},{1,9},{2,10},{3,11},{4,12},{5,13},{6,14},{7,15},{8,0},{9,1},... | collective-permute-start | bytes 589832 | tf_op jit(solution)/shard_map/ppermute | solution.py:47
  62.4 8.4 %collective-permute-start.17 = (bf16[128,768]{1,0:T(8,128)(2,1)S(1)}, bf16[128,768]{1,0:T(8,128)(2,1)S(1)}, u32[]{:S(2)}, u32[]{:S(2)}) collective-permute-start(bf16[128,768]{1,0:T(8,128)(2,1)S(1)} %get-tuple-element.103), channel_id=1, source_target_pairs={{0,2},{1,3},{2,4},{3,5},{4,6},{5,7},{6,0},{7,1},{8,10},{9,11},{10,... | collective-permute-start | bytes 589832 | tf_op jit(solution)/shard_map/ppermute | solution.py:47
  62.5 8.4 %collective-permute-start.18 = (bf16[128,768]{1,0:T(8,128)(2,1)S(1)}, bf16[128,768]{1,0:T(8,128)(2,1)S(1)}, u32[]{:S(2)}, u32[]{:S(2)}) collective-permute-start(bf16[128,768]{1,0:T(8,128)(2,1)S(1)} %get-tuple-element.102), channel_id=1, source_target_pairs={{0,6},{1,7},{2,0},{3,1},{4,2},{5,3},{6,4},{7,5},{8,14},{9,15},{10,... | collective-permute-start | bytes 589832 | tf_op jit(solution)/shard_map/ppermute | solution.py:47
  72.1 13.8 %collective-permute-start.23 = (bf16[128,2304]{1,0:T(8,128)(2,1)S(1)}, bf16[128,2304]{1,0:T(8,128)(2,1)S(1)}, u32[]{:S(2)}, u32[]{:S(2)}) collective-permute-start(bf16[128,2304]{1,0:T(8,128)(2,1)S(1)} %get-tuple-element.100), channel_id=1, source_target_pairs={{0,8},{1,9},{2,10},{3,11},{4,12},{5,13},{6,14},{7,15},{8,0},{9,1},... | collective-permute-start | bytes 1769480 | tf_op jit(solution)/shard_map/ppermute | solution.py:47
  73.7 13.4 %collective-permute-start.24 = (bf16[128,2304]{1,0:T(8,128)(2,1)S(1)}, bf16[128,2304]{1,0:T(8,128)(2,1)S(1)}, u32[]{:S(2)}, u32[]{:S(2)}) collective-permute-start(bf16[128,2304]{1,0:T(8,128)(2,1)S(1)} %get-tuple-element.99), channel_id=1, source_target_pairs={{0,6},{1,7},{2,0},{3,1},{4,2},{5,3},{6,4},{7,5},{8,14},{9,15},{10,... | collective-permute-start | bytes 1769480 | tf_op jit(solution)/shard_map/ppermute | solution.py:47
  75.3 14.5 %collective-permute-start.25 = (bf16[128,2304]{1,0:T(8,128)(2,1)S(1)}, bf16[128,2304]{1,0:T(8,128)(2,1)S(1)}, u32[]{:S(2)}, u32[]{:S(2)}) collective-permute-start(bf16[128,2304]{1,0:T(8,128)(2,1)S(1)} %get-tuple-element.98), channel_id=1, source_target_pairs={{0,2},{1,3},{2,4},{3,5},{4,6},{5,7},{6,0},{7,1},{8,10},{9,11},{10,... | collective-permute-start | bytes 1769480 | tf_op jit(solution)/shard_map/ppermute | solution.py:47
  90.3 15.7 %collective-permute-start.26 = (bf16[128,2304]{1,0:T(8,128)(2,1)S(1)}, bf16[128,2304]{1,0:T(8,128)(2,1)S(1)}, u32[]{:S(2)}, u32[]{:S(2)}) collective-permute-start(bf16[128,2304]{1,0:T(8,128)(2,1)S(1)} %slice.69), channel_id=1, source_target_pairs={{0,6},{1,7},{2,0},{3,1},{4,2},{5,3},{6,4},{7,5},{8,14},{9,15},{10,... | collective-permute-start | bytes 1769480 | tf_op jit(solution)/shard_map/ppermute | solution.py:47
  90.6 16.6 %collective-permute-start.27 = (bf16[128,2304]{1,0:T(8,128)(2,1)S(1)}, bf16[128,2304]{1,0:T(8,128)(2,1)S(1)}, u32[]{:S(2)}, u32[]{:S(2)}) collective-permute-start(bf16[128,2304]{1,0:T(8,128)(2,1)S(1)} %get-tuple-element.87), channel_id=1, source_target_pairs={{0,2},{1,3},{2,4},{3,5},{4,6},{5,7},{6,0},{7,1},{8,10},{9,11},{10,... | collective-permute-start | bytes 1769480 | tf_op jit(solution)/shard_map/ppermute | solution.py:47
  92.4 15.1 %collective-permute-start.28 = (bf16[128,2304]{1,0:T(8,128)(2,1)S(1)}, bf16[128,2304]{1,0:T(8,128)(2,1)S(1)}, u32[]{:S(2)}, u32[]{:S(2)}) collective-permute-start(bf16[128,2304]{1,0:T(8,128)(2,1)S(1)} %get-tuple-element.88), channel_id=1, source_target_pairs={{0,8},{1,9},{2,10},{3,11},{4,12},{5,13},{6,14},{7,15},{8,0},{9,1},... | collective-permute-start | bytes 1769480 | tf_op jit(solution)/shard_map/ppermute | solution.py:47
  (12 other events, 106.2 us)

commit v3 on v2

--- a/solution.py
+++ b/solution.py
@@ -56,14 +56,14 @@
 
 
 def turn_kernel(pre_act, hidden):
-    hidden[...] = gelu_parts(pre_act[...].astype(f32))[0].T.astype(bf16)
+    hidden[...] = gelu_parts(pre_act[...].astype(f32))[0].astype(bf16).T
 
 
 def slope_kernel(pre_act, slopes):
     slopes[...] = gelu_parts(pre_act[...].astype(f32))[1]
 
 
-def local(kernel, pre_act, turn, dtype, cost, tile=768):
+def local(kernel, pre_act, turn, dtype, cost, tile=1152):
     rows, units = pre_act.shape
     across = pl.BlockSpec((rows, tile), lambda j: (0, j))
     along = pl.BlockSpec((tile, rows), lambda j: (j, 0))
@@ -215,21 +215,20 @@
     both = jnp.stack([cotangent, partner])
     up, down = [both], [both]
     weight = jnp.concatenate([down_weight, weight], axis=1)
-    slopes = local(slope_kernel, pre_act, False, f32, 16 << 20)
     for n in range(3):
         up.append(move_mp(up[-1], 0, 1))
         down.append(move_mp(down[-1], 0, -1))
         if n == 0:
-            up[1], down[1], weight, slopes = barrier((up[1], down[1], weight, slopes))
+            up[1], down[1], weight = barrier((up[1], down[1], weight))
     x_other = move_dp(hidden, 1, 0, 0)
     y_prev = move_dp(hidden, 0, 1, 0)
     y_next = move_dp(hidden, 0, -1, 0)
     x_other, y_prev = barrier((x_other, y_prev))
+    y_far = move_dp(y_next, 0, -1, 0)
+    xy_prev = move_dp(x_other, 0, 1, 0)
     xy_next = move_dp(y_next, 1, 0, 0)
-    xy_prev = move_dp(x_other, 0, 1, 0)
-    y_far = move_dp(y_next, 0, -1, 0)
-    up[3], down[3], xy_next, xy_prev, y_far = barrier(
-        (up[3], down[3], xy_next, xy_prev, y_far)
+    up[3], down[3], y_far, xy_prev, xy_next = barrier(
+        (up[3], down[3], y_far, xy_prev, xy_next)
     )
     size = units // 3
     cut = lambda x, i: x[i * size : (i + 1) * size]
@@ -251,17 +250,17 @@
             ).astype(bf16)
         )
 
-    split = lambda x: [x[k * rows : (k + 1) * rows] for k in range(4)]
+    split = lambda x: [x[k * rows : (k + 1) * rows] for k in range(7)]
     third = lambda x, i: x[:, i * size : (i + 1) * size]
-    p_far, p_xy_next, p_xy_prev, p_y_far = split(partial(0, 4))
+    p_far = partial(0, 1)
     got0 = move_dp(third(p_far, 0), 0, 1, 0)
     got1 = move_dp(third(p_far, 1), 0, -1, 0)
     got2 = move_dp(third(p_far, 2), 1, 0, 0)
-    near = partial(4, 8)
-    got0, got1, got2, near, cot_wide, xy_far = barrier(
-        (got0, got1, got2, near, cot_wide, xy_far)
-    )
-    p_next, p_prev, p_x, p_mine = split(near)
+    rest = partial(1, 8)
+    got0, got1, got2, rest, cot_wide, xy_far = barrier(
+        (got0, got1, got2, rest, cot_wide, xy_far)
+    )
+    p_xy_next, p_xy_prev, p_y_far, p_next, p_prev, p_x, p_mine = split(rest)
     got_x = move_dp(add_third(p_xy_next, 0, got0), 1, 0, 0)
     got_m = move_dp(add_third(p_xy_prev, 1, got1), 0, -1, 0)
     got_y = move_dp(add_third(p_y_far, 2, got2), 0, 1, 0)
@@ -275,7 +274,9 @@
     end_x = move_dp(p_x, 1, 0, 0)
     end_prev = move_dp(p_prev, 0, -1, 0)
     step_update = adam(grad_own, swap(grad_give), first_moment, second_moment, units // 6)
-    end_prev, end_next, end_x, step_update = barrier((end_prev, end_next, end_x, step_update))
+    step_update, pre_act = barrier((step_update, pre_act))
+    slopes = local(slope_kernel, pre_act, False, f32, 1)
+    end_prev, end_next, end_x, slopes = barrier((end_prev, end_next, end_x, slopes))
 
     hidden_grad = sum(t.astype(f32) for t in (p_mine, end_prev, end_next, end_x))
     return ((hidden_grad * slopes).astype(bf16), step_update)

time: 109 us -> 107 us (0.982)
  waiting for transfers between devices: 36 us -> 30.4 us
  other arithmetic: 4.87 us -> 7.21 us
  Pallas kernels: 20.4 us -> 18.9 us
  starting transfers between devices: 36.3 us -> 37.8 us
    ppermute x21, waiting for transfers between devices: 21.5 us -> 16.2 us  [move_dp(): return lax.ppermute(x, 'dp', pairs)]
    pallas_call x2, Pallas kernels: 6.34 us -> 4.82 us  [local(): pl.pallas_call(kernel, grid=(units // tile,), in_specs=[across], out_spec...]
    ppermute x21, starting transfers between devices: 23.5 us -> 25 us  [move_dp(): return lax.ppermute(x, 'dp', pairs)]
    convert_element_type x1, other arithmetic: 1.14 us -> 2.56 us  [shards(): return ((hidden_grad * slopes).astype(bf16), step_update)]
    unnamed x13 -> x11, local copies, waits for them, and re-layouts: 2.81 us -> 2.81 us
  transfers between devices with their start and end apart: 30 -> 30, of which waited for: 16 -> 13; matrix products, arithmetic and copies ran while one was open for 10% -> 12% of each run, Pallas kernels for 18% -> 17%
where the time goes in v3:
time: 107 us; the launch traced here: 106 us
  starting transfers between devices  37.8 us (35%)
  waiting for transfers between devices  30.4 us (28%)
  Pallas kernels  18.9 us (18%)
  matrix products  7.79 us (7%)
  other arithmetic  7.21 us (7%)
  local copies, waits for them, and re-layouts  3.19 us (3%)
    ppermute x21, starting transfers between devices, move_dp(): return lax.ppermute(x, 'dp', pairs)  25 us
    ppermute x21, waiting for transfers between devices, move_dp(): return lax.ppermute(x, 'dp', pairs)  16.2 us
    ppermute x9, waiting for transfers between devices, move_mp(): return lax.ppermute(x, 'mp', pairs)  14.2 us
    ppermute x9, starting transfers between devices, move_mp(): return lax.ppermute(x, 'mp', pairs)  12.7 us
    pallas_call x1, Pallas kernels, gradients(): pl.pallas_call(functools.partial(gradient_kernel, len(thirds), per), grid...  7.92 us
    dot_general x2, matrix products, partial(): lax.dot_general(cot_wide[lo * rows:hi * rows], weight, contract_cols, pre...  7.79 us
    pallas_call x1, Pallas kernels, adam(): pl.pallas_call(adam_kernel, grid=(units // tile,), in_specs=[block] * 4,...  5.12 us
    pallas_call x2, Pallas kernels, local(): pl.pallas_call(kernel, grid=(units // tile,), in_specs=[across], out_spec...  4.82 us
  transfers between devices with their start and end apart: 30, of which 13 were waited for; matrix products, arithmetic and copies ran while one was open for 12% of the time, Pallas kernels for 17%

profile of v3, /device:TPU:96, one launch (start us, length us, event | category | flops | bytes accessed | tf_op | source)
XLA Modules:
  0.0 106.1 jit_solution(15930704546712916912)
XLA Ops:
  0.7 3.1 %collective-permute-start = (bf16[128,640]{1,0:T(8,128)(2,1)}, bf16[128,640]{1,0:T(8,128)(2,1)S(1)}, u32[]{:S(2)}, u32[]{:S(2)}) collective-permute-start(bf16[128,640]{1,0:T(8,128)(2,1)} %param.6), channel_id=1, source_target_pairs={{0,128},{16,144},{32,160},{48,176},{64,192},{80,208},{96,224},{112... | collective-permute-start | bytes 491528 | tf_op jit(solution)/shard_map/ppermute | solution.py:52
  3.8 2.2 %shard_map.68.refs_9_ = bf16[2304,128]{1,0:T(8,128)(2,1)} custom-call(bf16[128,2304]{1,0:T(8,128)(2,1)} %pre_act.2), custom_call_target="tpu_custom_call" | custom-call | flops 5898240 | bytes 33554432 | tf_op jit(solution)/shard_map/pallas_call | solution.py:70
  10.9 3.2 %collective-permute-start.1 = (bf16[2,128,640]{2,1,0:T(8,128)(2,1)S(1)}, bf16[2,128,640]{2,1,0:T(8,128)(2,1)S(1)}, u32[]{:S(2)}, u32[]{:S(2)}) collective-permute-start(bf16[2,128,640]{2,1,0:T(8,128)(2,1)S(1)} %pad_maximum_fusion.1.refs_0_), channel_id=1, source_target_pairs={{0,16},{16,32},{32,48},{48,64},{64,80},{80,96},{96,112},{112,0},{1... | collective-permute-start | bytes 983048 | tf_op jit(solution)/shard_map/ppermute | solution.py:52
  14.1 3.2 %pad_maximum_fusion = bf16[2304,1280]{1,0:T(8,128)(2,1)S(1)} fusion(bf16[2304,640]{1,0:T(8,128)(2,1)} %collective-permute-done.3, bf16[2304,640]{1,0:T(8,128)(2,1)} %param.7), kind=kLoop, calls=%fused_computation | loop fusion | flops 11796480 | bytes 11796480 | tf_op jit(solution)/shard_map/concatenate | solution.py:217
  17.3 3.3 %collective-permute-done.1.refs_4_ = bf16[2,128,640]{2,1,0:T(8,128)(2,1)S(1)} collective-permute-done((bf16[2,128,640]{2,1,0:T(8,128)(2,1)S(1)}, bf16[2,128,640]{2,1,0:T(8,128)(2,1)S(1)}, u32[]{:S(2)}, u32[]{:S(2)}) %collective-permute-start.1) | collective-permute-done | bytes 327712 | tf_op jit(solution)/shard_map/ppermute | solution.py:52
  20.6 3.4 %collective-permute-done.2.refs_1_ = bf16[2,128,640]{2,1,0:T(8,128)(2,1)S(1)} collective-permute-done((bf16[2,128,640]{2,1,0:T(8,128)(2,1)S(1)}, bf16[2,128,640]{2,1,0:T(8,128)(2,1)S(1)}, u32[]{:S(2)}, u32[]{:S(2)}) %collective-permute-start.2) | collective-permute-done | bytes 327712 | tf_op jit(solution)/shard_map/ppermute | solution.py:52
  28.5 2.2 %collective-permute-start.9 = (bf16[2304,128]{1,0:T(8,128)(2,1)S(1)}, bf16[2304,128]{1,0:T(8,128)(2,1)S(1)}, u32[]{:S(2)}, u32[]{:S(2)}) collective-permute-start(bf16[2304,128]{1,0:T(8,128)(2,1)S(1)} %collective-permute-done.8.refs_6_), channel_id=1, source_target_pairs={{0,6},{1,7},{2,0},{3,1},{4,2},{5,3},{6,4},{7,5},{8,14},{9,15},{10,... | collective-permute-start | bytes 1769480 | tf_op jit(solution)/shard_map/ppermute | solution.py:47
  33.9 6.2 %collective-permute-done.12.refs_4_ = bf16[2304,128]{1,0:T(8,128)(2,1)S(1)} collective-permute-done((bf16[2304,128]{1,0:T(8,128)(2,1)S(1)}, bf16[2304,128]{1,0:T(8,128)(2,1)S(1)}, u32[]{:S(2)}, u32[]{:S(2)}) %collective-permute-start.12) | collective-permute-done | bytes 589856 | tf_op jit(solution)/shard_map/ppermute | solution.py:47
  42.5 1.8 %collective-permute-start.15 = (bf16[1,128,640]{2,1,0:T(8,128)(2,1)S(1)}, bf16[1,128,640]{2,1,0:T(8,128)(2,1)S(1)}, u32[]{:S(2)}, u32[]{:S(2)}) collective-permute-start(bf16[1,128,640]{2,1,0:T(8,128)(2,1)S(1)} %slice.52), channel_id=1, source_target_pairs={{0,112},{16,0},{32,16},{48,32},{64,48},{80,64},{96,80},{112,96},{1... | collective-permute-start | bytes 491528 | tf_op jit(solution)/shard_map/ppermute | solution.py:52
  44.3 3.0 %collective-permute-done.14.refs_7_ = bf16[1,128,640]{2,1,0:T(8,128)(2,1)S(1)} collective-permute-done((bf16[1,128,640]{2,1,0:T(8,128)(2,1)S(1)}, bf16[1,128,640]{2,1,0:T(8,128)(2,1)S(1)}, u32[]{:S(2)}, u32[]{:S(2)}) %collective-permute-start.14) | collective-permute-done | bytes 163872 | tf_op jit(solution)/shard_map/ppermute | solution.py:52
  47.3 2.0 %collective-permute-done.15.refs_8_ = bf16[1,128,640]{2,1,0:T(8,128)(2,1)S(1)} collective-permute-done((bf16[1,128,640]{2,1,0:T(8,128)(2,1)S(1)}, bf16[1,128,640]{2,1,0:T(8,128)(2,1)S(1)}, u32[]{:S(2)}, u32[]{:S(2)}) %collective-permute-start.15) | collective-permute-done | bytes 163872 | tf_op jit(solution)/shard_map/ppermute | solution.py:52
  50.4 3.8 %collective-permute-start.20 = (bf16[768,128]{1,0:T(8,128)(2,1)S(1)}, bf16[768,128]{1,0:T(8,128)(2,1)S(1)}, u32[]{:S(2)}, u32[]{:S(2)}) collective-permute-start(bf16[768,128]{1,0:T(8,128)(2,1)S(1)} %slice.58), channel_id=1, source_target_pairs={{0,6},{1,7},{2,0},{3,1},{4,2},{5,3},{6,4},{7,5},{8,14},{9,15},{10,... | collective-permute-start | bytes 589832 | tf_op jit(solution)/shard_map/ppermute | solution.py:47
  55.4 2.0 %convolution_convert_fusion.1 = bf16[128,2304]{1,0:T(8,128)(2,1)S(1)} fusion(bf16[2304,1280]{1,0:T(8,128)(2,1)S(1)} %pad_maximum_fusion, bf16[1024,1280]{1,0:T(8,128)(2,1)S(1)} %constant_dynamic-update-slice_fusion.refs_10_), kind=kOutput, calls=%fused_computation.2 | convolution fusion | flops 755269632 | bytes 6815744 | tf_op jit(solution)/shard_map/dot_general | solution.py:248
  57.8 3.0 %collective-permute-start.18 = (bf16[128,768]{1,0:T(8,128)(2,1)S(1)}, bf16[128,768]{1,0:T(8,128)(2,1)S(1)}, u32[]{:S(2)}, u32[]{:S(2)}) collective-permute-start(bf16[128,768]{1,0:T(8,128)(2,1)S(1)} %get-tuple-element.104), channel_id=1, source_target_pairs={{0,6},{1,7},{2,0},{3,1},{4,2},{5,3},{6,4},{7,5},{8,14},{9,15},{10,... | collective-permute-start | bytes 589832 | tf_op jit(solution)/shard_map/ppermute | solution.py:47
  62.3 5.8 %convolution_convert_fusion = bf16[896,2304]{1,0:T(8,128)(2,1)S(1)} fusion(bf16[2304,1280]{1,0:T(8,128)(2,1)S(1)} %pad_maximum_fusion, bf16[1024,1280]{1,0:T(8,128)(2,1)S(1)} %constant_dynamic-update-slice_fusion.refs_10_), kind=kOutput, calls=%fused_computation.1 | convolution fusion | flops 5286887424 | bytes 12320768 | tf_op jit(solution)/shard_map/dot_general | solution.py:248
  69.0 1.9 %collective-permute-start.24 = (bf16[128,2304]{1,0:T(8,128)(2,1)S(1)}, bf16[128,2304]{1,0:T(8,128)(2,1)S(1)}, u32[]{:S(2)}, u32[]{:S(2)}) collective-permute-start(bf16[128,2304]{1,0:T(8,128)(2,1)S(1)} %get-tuple-element.101), channel_id=1, source_target_pairs={{0,6},{1,7},{2,0},{3,1},{4,2},{5,3},{6,4},{7,5},{8,14},{9,15},{10,... | collective-permute-start | bytes 1769480 | tf_op jit(solution)/shard_map/ppermute | solution.py:47
  71.1 7.9 %shard_map.70 = (f32[2304,640]{1,0:T(8,128)}, bf16[2304,640]{1,0:T(8,128)(2,1)S(1)}) custom-call(bf16[768,128]{1,0:T(8,128)(2,1)S(1)} %collective-permute-done.20.refs_0_, bf16[768,128]{1,0:T(8,128)(2,1)S(1)} %collective-permute-done.21.refs_1_, bf16[768,128]{1,0:T(8,128)(2,1)S(1)} %collective-permute-done.22.refs_2_, ...), custom_call_target="tpu_custom_call" | custom-call | flops 6039797760 | bytes 18874368 | tf_op jit(solution)/shard_map/pallas_call | solution.py:109
  79.0 3.7 %collective-permute-done.23 = bf16[128,2304]{1,0:T(8,128)(2,1)S(1)} collective-permute-done((bf16[128,2304]{1,0:T(8,128)(2,1)S(1)}, bf16[128,2304]{1,0:T(8,128)(2,1)S(1)}, u32[]{:S(2)}, u32[]{:S(2)}) %collective-permute-start.23) | collective-permute-done | bytes 589856 | tf_op jit(solution)/shard_map/ppermute | solution.py:47
  83.0 3.1 %collective-permute-done.25 = bf16[128,2304]{1,0:T(8,128)(2,1)S(1)} collective-permute-done((bf16[128,2304]{1,0:T(8,128)(2,1)S(1)}, bf16[128,2304]{1,0:T(8,128)(2,1)S(1)}, u32[]{:S(2)}, u32[]{:S(2)}) %collective-permute-start.25) | collective-permute-done | bytes 589856 | tf_op jit(solution)/shard_map/ppermute | solution.py:47
  87.7 3.1 %collective-permute-start.26 = (bf16[128,2304]{1,0:T(8,128)(2,1)S(1)}, bf16[128,2304]{1,0:T(8,128)(2,1)S(1)}, u32[]{:S(2)}, u32[]{:S(2)}) collective-permute-start(bf16[128,2304]{1,0:T(8,128)(2,1)S(1)} %slice.65), channel_id=1, source_target_pairs={{0,6},{1,7},{2,0},{3,1},{4,2},{5,3},{6,4},{7,5},{8,14},{9,15},{10,... | collective-permute-start | bytes 1769480 | tf_op jit(solution)/shard_map/ppermute | solution.py:47
  92.0 2.7 %copy-done = f32[2304,640]{1,0:T(8,128)S(1)} copy-done((f32[2304,640]{1,0:T(8,128)S(1)}, f32[2304,640]{1,0:T(8,128)}, u32[]{:S(2)}) %copy-start) | copy-done | bytes 5898264
  94.6 5.1 %shard_map.71 = bf16[2304,640]{1,0:T(8,128)(2,1)} custom-call(f32[2304,640]{1,0:T(8,128)S(1)} %copy-done, bf16[2304,640]{1,0:T(8,128)(2,1)S(1)} %collective-permute-done.29.got, bf16[2304,640]{1,0:T(8,128)(2,1)S(1)} %copy-done.1, bf16[2304,640]{1,0:T(8,128)(2,1)S(1)} %copy-done.2), custom_call_target="tpu_custom_call" | custom-call | bytes 17694720 | tf_op jit(solution)/shard_map/pallas_call | solution.py:133
  99.8 2.6 %shard_map.72 = f32[128,2304]{1,0:T(8,128)} custom-call(bf16[128,2304]{1,0:T(8,128)(2,1)} %pre_act.2), custom_call_target="tpu_custom_call" | custom-call | flops 5898240 | bytes 1 | tf_op jit(solution)/shard_map/pallas_call | solution.py:70
  103.6 2.6 %multiply_convert_fusion = bf16[128,2304]{1,0:T(8,128)(2,1)} fusion(f32[128,2304]{1,0:T(8,128)} %shard_map.72, bf16[128,2304]{1,0:T(8,128)(2,1)S(1)} %collective-permute-done.28, bf16[128,2304]{1,0:T(8,128)(2,1)S(1)} %collective-permute-done.27, bf16[128,2304]{1,0:T(8,128)(2,1)S(1)} %collective-permute-done.26, bf16[896,2304]{1,0:T(8,128)(2,1)} %copy-done.4), kind=kLoop, calls=%fused_computation.4 | loop fusion | flops 2654208 | bytes 4128768 | tf_op jit(solution)/shard_map/convert_element_type | solution.py:282
  (68 shorter events, 24.3 us)
Async XLA Ops:
  0.6 13.5 %collective-permute-start.3 = (bf16[2304,640]{1,0:T(8,128)(2,1)}, bf16[2304,640]{1,0:T(8,128)(2,1)}, u32[]{:S(2)}, u32[]{:S(2)}) collective-permute-start(bf16[2304,640]{1,0:T(8,128)(2,1)} %param.7), channel_id=1, source_target_pairs={{0,1},{1,0},{2,3},{3,2},{4,5},{5,4},{6,7},{7,6},{8,9},{9,8},{10,11... | collective-permute-start | bytes 8847368 | tf_op jit(solution)/shard_map/ppermute | solution.py:47
  0.7 9.2 %collective-permute-start = (bf16[128,640]{1,0:T(8,128)(2,1)}, bf16[128,640]{1,0:T(8,128)(2,1)S(1)}, u32[]{:S(2)}, u32[]{:S(2)}) collective-permute-start(bf16[128,640]{1,0:T(8,128)(2,1)} %param.6), channel_id=1, source_target_pairs={{0,128},{16,144},{32,160},{48,176},{64,192},{80,208},{96,224},{112... | collective-permute-start | bytes 491528 | tf_op jit(solution)/shard_map/ppermute | solution.py:52
  6.1 20.0 %collective-permute-start.10 = (bf16[2304,128]{1,0:T(8,128)(2,1)}, bf16[2304,128]{1,0:T(8,128)(2,1)S(1)}, u32[]{:S(2)}, u32[]{:S(2)}) collective-permute-start(bf16[2304,128]{1,0:T(8,128)(2,1)} %shard_map.68.refs_9_), channel_id=1, source_target_pairs={{0,8},{1,9},{2,10},{3,11},{4,12},{5,13},{6,14},{7,15},{8,0},{9,1},... | collective-permute-start | bytes 1769480 | tf_op jit(solution)/shard_map/ppermute | solution.py:47
  6.7 19.4 %collective-permute-start.11 = (bf16[2304,128]{1,0:T(8,128)(2,1)}, bf16[2304,128]{1,0:T(8,128)(2,1)S(1)}, u32[]{:S(2)}, u32[]{:S(2)}) collective-permute-start(bf16[2304,128]{1,0:T(8,128)(2,1)} %shard_map.68.refs_9_), channel_id=1, source_target_pairs={{0,2},{1,3},{2,4},{3,5},{4,6},{5,7},{6,0},{7,1},{8,10},{9,11},{10,... | collective-permute-start | bytes 1769480 | tf_op jit(solution)/shard_map/ppermute | solution.py:47
  8.2 18.8 %collective-permute-start.8 = (bf16[2304,128]{1,0:T(8,128)(2,1)}, bf16[2304,128]{1,0:T(8,128)(2,1)S(1)}, u32[]{:S(2)}, u32[]{:S(2)}) collective-permute-start(bf16[2304,128]{1,0:T(8,128)(2,1)} %shard_map.68.refs_9_), channel_id=1, source_target_pairs={{0,6},{1,7},{2,0},{3,1},{4,2},{5,3},{6,4},{7,5},{8,14},{9,15},{10,... | collective-permute-start | bytes 1769480 | tf_op jit(solution)/shard_map/ppermute | solution.py:47
  10.9 9.7 %collective-permute-start.1 = (bf16[2,128,640]{2,1,0:T(8,128)(2,1)S(1)}, bf16[2,128,640]{2,1,0:T(8,128)(2,1)S(1)}, u32[]{:S(2)}, u32[]{:S(2)}) collective-permute-start(bf16[2,128,640]{2,1,0:T(8,128)(2,1)S(1)} %pad_maximum_fusion.1.refs_0_), channel_id=1, source_target_pairs={{0,16},{16,32},{32,48},{48,64},{64,80},{80,96},{96,112},{112,0},{1... | collective-permute-start | bytes 983048 | tf_op jit(solution)/shard_map/ppermute | solution.py:52
  14.1 9.9 %collective-permute-start.2 = (bf16[2,128,640]{2,1,0:T(8,128)(2,1)S(1)}, bf16[2,128,640]{2,1,0:T(8,128)(2,1)S(1)}, u32[]{:S(2)}, u32[]{:S(2)}) collective-permute-start(bf16[2,128,640]{2,1,0:T(8,128)(2,1)S(1)} %pad_maximum_fusion.1.refs_0_), channel_id=1, source_target_pairs={{0,112},{16,0},{32,16},{48,32},{64,48},{80,64},{96,80},{112,96},{1... | collective-permute-start | bytes 983048 | tf_op jit(solution)/shard_map/ppermute | solution.py:52
  24.3 9.3 %collective-permute-start.4 = (bf16[2,128,640]{2,1,0:T(8,128)(2,1)S(1)}, bf16[2,128,640]{2,1,0:T(8,128)(2,1)S(1)}, u32[]{:S(2)}, u32[]{:S(2)}) collective-permute-start(bf16[2,128,640]{2,1,0:T(8,128)(2,1)S(1)} %collective-permute-done.2.refs_1_), channel_id=1, source_target_pairs={{0,112},{16,0},{32,16},{48,32},{64,48},{80,64},{96,80},{112,96},{1... | collective-permute-start | bytes 983048 | tf_op jit(solution)/shard_map/ppermute | solution.py:52
  26.1 14.1 %collective-permute-start.12 = (bf16[2304,128]{1,0:T(8,128)(2,1)S(1)}, bf16[2304,128]{1,0:T(8,128)(2,1)S(1)}, u32[]{:S(2)}, u32[]{:S(2)}) collective-permute-start(bf16[2304,128]{1,0:T(8,128)(2,1)S(1)} %collective-permute-done.10.refs_8_), channel_id=1, source_target_pairs={{0,2},{1,3},{2,4},{3,5},{4,6},{5,7},{6,0},{7,1},{8,10},{9,11},{10,... | collective-permute-start | bytes 1769480 | tf_op jit(solution)/shard_map/ppermute | solution.py:47
  27.0 13.1 %collective-permute-start.13 = (bf16[2304,128]{1,0:T(8,128)(2,1)S(1)}, bf16[2304,128]{1,0:T(8,128)(2,1)S(1)}, u32[]{:S(2)}, u32[]{:S(2)}) collective-permute-start(bf16[2304,128]{1,0:T(8,128)(2,1)S(1)} %collective-permute-done.8.refs_6_), channel_id=1, source_target_pairs={{0,8},{1,9},{2,10},{3,11},{4,12},{5,13},{6,14},{7,15},{8,0},{9,1},... | collective-permute-start | bytes 1769480 | tf_op jit(solution)/shard_map/ppermute | solution.py:47
  28.5 12.1 %collective-permute-start.9 = (bf16[2304,128]{1,0:T(8,128)(2,1)S(1)}, bf16[2304,128]{1,0:T(8,128)(2,1)S(1)}, u32[]{:S(2)}, u32[]{:S(2)}) collective-permute-start(bf16[2304,128]{1,0:T(8,128)(2,1)S(1)} %collective-permute-done.8.refs_6_), channel_id=1, source_target_pairs={{0,6},{1,7},{2,0},{3,1},{4,2},{5,3},{6,4},{7,5},{8,14},{9,15},{10,... | collective-permute-start | bytes 1769480 | tf_op jit(solution)/shard_map/ppermute | solution.py:47
  31.9 8.7 %collective-permute-start.6 = (bf16[2,128,640]{2,1,0:T(8,128)(2,1)S(1)}, bf16[2,128,640]{2,1,0:T(8,128)(2,1)S(1)}, u32[]{:S(2)}, u32[]{:S(2)}) collective-permute-start(bf16[2,128,640]{2,1,0:T(8,128)(2,1)S(1)} %collective-permute-done.5.refs_5_), channel_id=1, source_target_pairs={{0,16},{16,32},{32,48},{48,64},{64,80},{80,96},{96,112},{112,0},{1... | collective-permute-start | bytes 983048 | tf_op jit(solution)/shard_map/ppermute | solution.py:52
  33.6 8.3 %collective-permute-start.7 = (bf16[2,128,640]{2,1,0:T(8,128)(2,1)S(1)}, bf16[2,128,640]{2,1,0:T(8,128)(2,1)S(1)}, u32[]{:S(2)}, u32[]{:S(2)}) collective-permute-start(bf16[2,128,640]{2,1,0:T(8,128)(2,1)S(1)} %collective-permute-done.4.refs_2_), channel_id=1, source_target_pairs={{0,112},{16,0},{32,16},{48,32},{64,48},{80,64},{96,80},{112,96},{1... | collective-permute-start | bytes 983048 | tf_op jit(solution)/shard_map/ppermute | solution.py:52
  50.4 10.4 %collective-permute-start.20 = (bf16[768,128]{1,0:T(8,128)(2,1)S(1)}, bf16[768,128]{1,0:T(8,128)(2,1)S(1)}, u32[]{:S(2)}, u32[]{:S(2)}) collective-permute-start(bf16[768,128]{1,0:T(8,128)(2,1)S(1)} %slice.58), channel_id=1, source_target_pairs={{0,6},{1,7},{2,0},{3,1},{4,2},{5,3},{6,4},{7,5},{8,14},{9,15},{10,... | collective-permute-start | bytes 589832 | tf_op jit(solution)/shard_map/ppermute | solution.py:47
  54.2 13.8 %collective-permute-start.21 = (bf16[768,128]{1,0:T(8,128)(2,1)S(1)}, bf16[768,128]{1,0:T(8,128)(2,1)S(1)}, u32[]{:S(2)}, u32[]{:S(2)}) collective-permute-start(bf16[768,128]{1,0:T(8,128)(2,1)S(1)} %slice.59), channel_id=1, source_target_pairs={{0,2},{1,3},{2,4},{3,5},{4,6},{5,7},{6,0},{7,1},{8,10},{9,11},{10,... | collective-permute-start | bytes 589832 | tf_op jit(solution)/shard_map/ppermute | solution.py:47
  54.3 13.7 %collective-permute-start.22 = (bf16[768,128]{1,0:T(8,128)(2,1)S(1)}, bf16[768,128]{1,0:T(8,128)(2,1)S(1)}, u32[]{:S(2)}, u32[]{:S(2)}) collective-permute-start(bf16[768,128]{1,0:T(8,128)(2,1)S(1)} %slice.60), channel_id=1, source_target_pairs={{0,8},{1,9},{2,10},{3,11},{4,12},{5,13},{6,14},{7,15},{8,0},{9,1},... | collective-permute-start | bytes 589832 | tf_op jit(solution)/shard_map/ppermute | solution.py:47
  57.5 10.6 %collective-permute-start.17 = (bf16[128,768]{1,0:T(8,128)(2,1)S(1)}, bf16[128,768]{1,0:T(8,128)(2,1)S(1)}, u32[]{:S(2)}, u32[]{:S(2)}) collective-permute-start(bf16[128,768]{1,0:T(8,128)(2,1)S(1)} %get-tuple-element.105), channel_id=1, source_target_pairs={{0,2},{1,3},{2,4},{3,5},{4,6},{5,7},{6,0},{7,1},{8,10},{9,11},{10,... | collective-permute-start | bytes 589832 | tf_op jit(solution)/shard_map/ppermute | solution.py:47
  57.8 10.3 %collective-permute-start.18 = (bf16[128,768]{1,0:T(8,128)(2,1)S(1)}, bf16[128,768]{1,0:T(8,128)(2,1)S(1)}, u32[]{:S(2)}, u32[]{:S(2)}) collective-permute-start(bf16[128,768]{1,0:T(8,128)(2,1)S(1)} %get-tuple-element.104), channel_id=1, source_target_pairs={{0,6},{1,7},{2,0},{3,1},{4,2},{5,3},{6,4},{7,5},{8,14},{9,15},{10,... | collective-permute-start | bytes 589832 | tf_op jit(solution)/shard_map/ppermute | solution.py:47
  68.3 14.4 %collective-permute-start.23 = (bf16[128,2304]{1,0:T(8,128)(2,1)S(1)}, bf16[128,2304]{1,0:T(8,128)(2,1)S(1)}, u32[]{:S(2)}, u32[]{:S(2)}) collective-permute-start(bf16[128,2304]{1,0:T(8,128)(2,1)S(1)} %get-tuple-element.102), channel_id=1, source_target_pairs={{0,8},{1,9},{2,10},{3,11},{4,12},{5,13},{6,14},{7,15},{8,0},{9,1},... | collective-permute-start | bytes 1769480 | tf_op jit(solution)/shard_map/ppermute | solution.py:47
  69.0 14.0 %collective-permute-start.24 = (bf16[128,2304]{1,0:T(8,128)(2,1)S(1)}, bf16[128,2304]{1,0:T(8,128)(2,1)S(1)}, u32[]{:S(2)}, u32[]{:S(2)}) collective-permute-start(bf16[128,2304]{1,0:T(8,128)(2,1)S(1)} %get-tuple-element.101), channel_id=1, source_target_pairs={{0,6},{1,7},{2,0},{3,1},{4,2},{5,3},{6,4},{7,5},{8,14},{9,15},{10,... | collective-permute-start | bytes 1769480 | tf_op jit(solution)/shard_map/ppermute | solution.py:47
  70.9 15.2 %collective-permute-start.25 = (bf16[128,2304]{1,0:T(8,128)(2,1)S(1)}, bf16[128,2304]{1,0:T(8,128)(2,1)S(1)}, u32[]{:S(2)}, u32[]{:S(2)}) collective-permute-start(bf16[128,2304]{1,0:T(8,128)(2,1)S(1)} %get-tuple-element.100), channel_id=1, source_target_pairs={{0,2},{1,3},{2,4},{3,5},{4,6},{5,7},{6,0},{7,1},{8,10},{9,11},{10,... | collective-permute-start | bytes 1769480 | tf_op jit(solution)/shard_map/ppermute | solution.py:47
  86.6 17.0 %collective-permute-start.27 = (bf16[128,2304]{1,0:T(8,128)(2,1)S(1)}, bf16[128,2304]{1,0:T(8,128)(2,1)S(1)}, u32[]{:S(2)}, u32[]{:S(2)}) collective-permute-start(bf16[128,2304]{1,0:T(8,128)(2,1)S(1)} %get-tuple-element.88), channel_id=1, source_target_pairs={{0,2},{1,3},{2,4},{3,5},{4,6},{5,7},{6,0},{7,1},{8,10},{9,11},{10,... | collective-permute-start | bytes 1769480 | tf_op jit(solution)/shard_map/ppermute | solution.py:47
  86.7 16.9 %collective-permute-start.28 = (bf16[128,2304]{1,0:T(8,128)(2,1)S(1)}, bf16[128,2304]{1,0:T(8,128)(2,1)S(1)}, u32[]{:S(2)}, u32[]{:S(2)}) collective-permute-start(bf16[128,2304]{1,0:T(8,128)(2,1)S(1)} %get-tuple-element.89), channel_id=1, source_target_pairs={{0,8},{1,9},{2,10},{3,11},{4,12},{5,13},{6,14},{7,15},{8,0},{9,1},... | collective-permute-start | bytes 1769480 | tf_op jit(solution)/shard_map/ppermute | solution.py:47
  87.7 15.9 %collective-permute-start.26 = (bf16[128,2304]{1,0:T(8,128)(2,1)S(1)}, bf16[128,2304]{1,0:T(8,128)(2,1)S(1)}, u32[]{:S(2)}, u32[]{:S(2)}) collective-permute-start(bf16[128,2304]{1,0:T(8,128)(2,1)S(1)} %slice.65), channel_id=1, source_target_pairs={{0,6},{1,7},{2,0},{3,1},{4,2},{5,3},{6,4},{7,5},{8,14},{9,15},{10,... | collective-permute-start | bytes 1769480 | tf_op jit(solution)/shard_map/ppermute | solution.py:47
  (11 other events, 95.3 us)

commit v4 on v3

--- a/solution.py
+++ b/solution.py
@@ -73,6 +73,7 @@
         in_specs=[across],
         out_specs=along if turn else across,
         out_shape=jax.ShapeDtypeStruct((units, rows) if turn else (rows, units), dtype),
+        compiler_params=pltpu.CompilerParams(vmem_limit_bytes=12 << 20),
         cost_estimate=pl.CostEstimate(
             flops=20 * rows * units, bytes_accessed=cost, transcendentals=rows * units
         ),

time: 107 us -> 105 us (0.981)
  Pallas kernels: 18.9 us -> 15.6 us
  local copies, waits for them, and re-layouts: 3.19 us -> 5.43 us
  waiting for transfers between devices: 30.4 us -> 28.6 us
  other arithmetic: 7.21 us -> 8.37 us
    pallas_call x2, Pallas kernels: 4.82 us -> 1.53 us  [local(): pl.pallas_call(kernel, grid=(units // tile,), in_specs=[across], out_spec...]
    ppermute x9, waiting for transfers between devices: 14.2 us -> 11.7 us  [move_mp(): return lax.ppermute(x, 'mp', pairs)]
    concatenate x1, other arithmetic: 3.16 us -> 5.71 us  [shards(): weight = jnp.concatenate([down_weight, weight], axis=1)]
    unnamed x11 -> x13, local copies, waits for them, and re-layouts: 2.81 us -> 5.06 us
    convert_element_type x1, other arithmetic: 2.56 us -> 1.17 us  [shards(): return ((hidden_grad * slopes).astype(bf16), step_update)]
  transfers between devices with their start and end apart: 30 -> 30, of which waited for: 13 -> 14; matrix products, arithmetic and copies ran while one was open for 12% -> 14% of each run, Pallas kernels for 17% -> 14%
where the time goes in v4:
time: 105 us; the launch traced here: 104 us
  starting transfers between devices  37.8 us (36%)
  waiting for transfers between devices  28.6 us (27%)
  Pallas kernels  15.6 us (15%)
  other arithmetic  8.37 us (8%)
  matrix products  7.77 us (7%)
  local copies, waits for them, and re-layouts  5.43 us (5%)
    ppermute x21, starting transfers between devices, move_dp(): return lax.ppermute(x, 'dp', pairs)  25 us
    ppermute x21, waiting for transfers between devices, move_dp(): return lax.ppermute(x, 'dp', pairs)  17 us
    ppermute x9, starting transfers between devices, move_mp(): return lax.ppermute(x, 'mp', pairs)  12.7 us
    ppermute x9, waiting for transfers between devices, move_mp(): return lax.ppermute(x, 'mp', pairs)  11.7 us
    pallas_call x1, Pallas kernels, gradients(): pl.pallas_call(functools.partial(gradient_kernel, len(thirds), per), grid...  7.94 us
    dot_general x2, matrix products, partial(): lax.dot_general(cot_wide[lo * rows:hi * rows], weight, contract_cols, pre...  7.77 us
    concatenate x1, other arithmetic, shards(): weight = jnp.concatenate([down_weight, weight], axis=1)  5.71 us
    pallas_call x1, Pallas kernels, adam(): pl.pallas_call(adam_kernel, grid=(units // tile,), in_specs=[block] * 4,...  5.12 us
  transfers between devices with their start and end apart: 30, of which 14 were waited for; matrix products, arithmetic and copies ran while one was open for 14% of the time, Pallas kernels for 14%

profile of v4, /device:TPU:96, one launch (start us, length us, event | category | flops | bytes accessed | tf_op | source)
XLA Modules:
  0.0 104.4 jit_solution(8029765392690908648)
XLA Ops:
  0.7 3.1 %collective-permute-start = (bf16[128,640]{1,0:T(8,128)(2,1)}, bf16[128,640]{1,0:T(8,128)(2,1)S(1)}, u32[]{:S(2)}, u32[]{:S(2)}) collective-permute-start(bf16[128,640]{1,0:T(8,128)(2,1)} %param.6), channel_id=1, source_target_pairs={{0,128},{16,144},{32,160},{48,176},{64,192},{80,208},{96,224},{112... | collective-permute-start | bytes 491528 | tf_op jit(solution)/shard_map/ppermute | solution.py:52
  6.2 1.6 %collective-permute-start.11 = (bf16[2304,128]{1,0:T(8,128)(2,1)S(1)}, bf16[2304,128]{1,0:T(8,128)(2,1)S(1)}, u32[]{:S(2)}, u32[]{:S(2)}) collective-permute-start(bf16[2304,128]{1,0:T(8,128)(2,1)S(1)} %shard_map.68.refs_9_), channel_id=1, source_target_pairs={{0,2},{1,3},{2,4},{3,5},{4,6},{5,7},{6,0},{7,1},{8,10},{9,11},{10,... | collective-permute-start | bytes 1769480 | tf_op jit(solution)/shard_map/ppermute | solution.py:47
  7.8 1.7 %collective-permute-start.8 = (bf16[2304,128]{1,0:T(8,128)(2,1)S(1)}, bf16[2304,128]{1,0:T(8,128)(2,1)S(1)}, u32[]{:S(2)}, u32[]{:S(2)}) collective-permute-start(bf16[2304,128]{1,0:T(8,128)(2,1)S(1)} %shard_map.68.refs_9_), channel_id=1, source_target_pairs={{0,6},{1,7},{2,0},{3,1},{4,2},{5,3},{6,4},{7,5},{8,14},{9,15},{10,... | collective-permute-start | bytes 1769480 | tf_op jit(solution)/shard_map/ppermute | solution.py:47
  10.5 3.2 %collective-permute-start.1 = (bf16[2,128,640]{2,1,0:T(8,128)(2,1)S(1)}, bf16[2,128,640]{2,1,0:T(8,128)(2,1)S(1)}, u32[]{:S(2)}, u32[]{:S(2)}) collective-permute-start(bf16[2,128,640]{2,1,0:T(8,128)(2,1)S(1)} %pad_maximum_fusion.1.refs_0_), channel_id=1, source_target_pairs={{0,16},{16,32},{32,48},{48,64},{64,80},{80,96},{96,112},{112,0},{1... | collective-permute-start | bytes 983048 | tf_op jit(solution)/shard_map/ppermute | solution.py:52
  13.7 5.7 %pad_maximum_fusion = bf16[2304,1280]{1,0:T(8,128)(2,1)} fusion(bf16[2304,640]{1,0:T(8,128)(2,1)} %collective-permute-done.3, bf16[2304,640]{1,0:T(8,128)(2,1)} %param.7), kind=kLoop, calls=%fused_computation | loop fusion | flops 11796480 | bytes 11796480 | tf_op jit(solution)/shard_map/concatenate | solution.py:218
  20.2 3.4 %collective-permute-done.2.refs_1_ = bf16[2,128,640]{2,1,0:T(8,128)(2,1)S(1)} collective-permute-done((bf16[2,128,640]{2,1,0:T(8,128)(2,1)S(1)}, bf16[2,128,640]{2,1,0:T(8,128)(2,1)S(1)}, u32[]{:S(2)}, u32[]{:S(2)}) %collective-permute-start.2) | collective-permute-done | bytes 327712 | tf_op jit(solution)/shard_map/ppermute | solution.py:52
  23.9 1.7 %collective-permute-start.4 = (bf16[2,128,640]{2,1,0:T(8,128)(2,1)S(1)}, bf16[2,128,640]{2,1,0:T(8,128)(2,1)S(1)}, u32[]{:S(2)}, u32[]{:S(2)}) collective-permute-start(bf16[2,128,640]{2,1,0:T(8,128)(2,1)S(1)} %collective-permute-done.2.refs_1_), channel_id=1, source_target_pairs={{0,112},{16,0},{32,16},{48,32},{64,48},{80,64},{96,80},{112,96},{1... | collective-permute-start | bytes 983048 | tf_op jit(solution)/shard_map/ppermute | solution.py:52
  27.0 1.5 %collective-permute-start.13 = (bf16[2304,128]{1,0:T(8,128)(2,1)S(1)}, bf16[2304,128]{1,0:T(8,128)(2,1)S(1)}, u32[]{:S(2)}, u32[]{:S(2)}) collective-permute-start(bf16[2304,128]{1,0:T(8,128)(2,1)S(1)} %collective-permute-done.8.refs_6_), channel_id=1, source_target_pairs={{0,8},{1,9},{2,10},{3,11},{4,12},{5,13},{6,14},{7,15},{8,0},{9,1},... | collective-permute-start | bytes 1769480 | tf_op jit(solution)/shard_map/ppermute | solution.py:47
  28.5 1.8 %collective-permute-start.9 = (bf16[2304,128]{1,0:T(8,128)(2,1)S(1)}, bf16[2304,128]{1,0:T(8,128)(2,1)S(1)}, u32[]{:S(2)}, u32[]{:S(2)}) collective-permute-start(bf16[2304,128]{1,0:T(8,128)(2,1)S(1)} %collective-permute-done.8.refs_6_), channel_id=1, source_target_pairs={{0,6},{1,7},{2,0},{3,1},{4,2},{5,3},{6,4},{7,5},{8,14},{9,15},{10,... | collective-permute-start | bytes 1769480 | tf_op jit(solution)/shard_map/ppermute | solution.py:47
  31.5 1.7 %collective-permute-start.6 = (bf16[2,128,640]{2,1,0:T(8,128)(2,1)S(1)}, bf16[2,128,640]{2,1,0:T(8,128)(2,1)S(1)}, u32[]{:S(2)}, u32[]{:S(2)}) collective-permute-start(bf16[2,128,640]{2,1,0:T(8,128)(2,1)S(1)} %collective-permute-done.5.refs_5_), channel_id=1, source_target_pairs={{0,16},{16,32},{32,48},{48,64},{64,80},{80,96},{96,112},{112,0},{1... | collective-permute-start | bytes 983048 | tf_op jit(solution)/shard_map/ppermute | solution.py:52
  33.5 6.3 %collective-permute-done.12.refs_4_ = bf16[2304,128]{1,0:T(8,128)(2,1)S(1)} collective-permute-done((bf16[2304,128]{1,0:T(8,128)(2,1)S(1)}, bf16[2304,128]{1,0:T(8,128)(2,1)S(1)}, u32[]{:S(2)}, u32[]{:S(2)}) %collective-permute-start.12) | collective-permute-done | bytes 589856 | tf_op jit(solution)/shard_map/ppermute | solution.py:47
  43.8 3.0 %collective-permute-done.14.refs_7_ = bf16[1,128,640]{2,1,0:T(8,128)(2,1)S(1)} collective-permute-done((bf16[1,128,640]{2,1,0:T(8,128)(2,1)S(1)}, bf16[1,128,640]{2,1,0:T(8,128)(2,1)S(1)}, u32[]{:S(2)}, u32[]{:S(2)}) %collective-permute-start.14) | collective-permute-done | bytes 163872 | tf_op jit(solution)/shard_map/ppermute | solution.py:52
  46.8 2.4 %collective-permute-done.15.refs_8_ = bf16[1,128,640]{2,1,0:T(8,128)(2,1)S(1)} collective-permute-done((bf16[1,128,640]{2,1,0:T(8,128)(2,1)S(1)}, bf16[1,128,640]{2,1,0:T(8,128)(2,1)S(1)}, u32[]{:S(2)}, u32[]{:S(2)}) %collective-permute-start.15) | collective-permute-done | bytes 163872 | tf_op jit(solution)/shard_map/ppermute | solution.py:52
  50.4 3.2 %collective-permute-start.20 = (bf16[768,128]{1,0:T(8,128)(2,1)S(1)}, bf16[768,128]{1,0:T(8,128)(2,1)S(1)}, u32[]{:S(2)}, u32[]{:S(2)}) collective-permute-start(bf16[768,128]{1,0:T(8,128)(2,1)S(1)} %slice.58), channel_id=1, source_target_pairs={{0,6},{1,7},{2,0},{3,1},{4,2},{5,3},{6,4},{7,5},{8,14},{9,15},{10,... | collective-permute-start | bytes 589832 | tf_op jit(solution)/shard_map/ppermute | solution.py:47
  56.3 2.0 %convolution_convert_fusion.1 = bf16[128,2304]{1,0:T(8,128)(2,1)S(1)} fusion(bf16[2304,1280]{1,0:T(8,128)(2,1)S(1)} %copy-done.5, bf16[1024,1280]{1,0:T(8,128)(2,1)S(1)} %constant_dynamic-update-slice_fusion.refs_10_), kind=kOutput, calls=%fused_computation.2 | convolution fusion | flops 755269632 | bytes 6815744 | tf_op jit(solution)/shard_map/dot_general | solution.py:249
  58.4 3.2 %collective-permute-start.18 = (bf16[128,768]{1,0:T(8,128)(2,1)S(1)}, bf16[128,768]{1,0:T(8,128)(2,1)S(1)}, u32[]{:S(2)}, u32[]{:S(2)}) collective-permute-start(bf16[128,768]{1,0:T(8,128)(2,1)S(1)} %get-tuple-element.104), channel_id=1, source_target_pairs={{0,6},{1,7},{2,0},{3,1},{4,2},{5,3},{6,4},{7,5},{8,14},{9,15},{10,... | collective-permute-start | bytes 589832 | tf_op jit(solution)/shard_map/ppermute | solution.py:47
  62.6 5.7 %convolution_convert_fusion = bf16[896,2304]{1,0:T(8,128)(2,1)S(1)} fusion(bf16[2304,1280]{1,0:T(8,128)(2,1)S(1)} %copy-done.5, bf16[1024,1280]{1,0:T(8,128)(2,1)S(1)} %constant_dynamic-update-slice_fusion.refs_10_), kind=kOutput, calls=%fused_computation.1 | convolution fusion | flops 5286887424 | bytes 12320768 | tf_op jit(solution)/shard_map/dot_general | solution.py:249
  71.8 7.9 %shard_map.70 = (f32[2304,640]{1,0:T(8,128)}, bf16[2304,640]{1,0:T(8,128)(2,1)S(1)}) custom-call(bf16[768,128]{1,0:T(8,128)(2,1)S(1)} %collective-permute-done.20.refs_0_, bf16[768,128]{1,0:T(8,128)(2,1)S(1)} %collective-permute-done.21.refs_1_, bf16[768,128]{1,0:T(8,128)(2,1)S(1)} %collective-permute-done.22.refs_2_, ...), custom_call_target="tpu_custom_call" | custom-call | flops 6039797760 | bytes 18874368 | tf_op jit(solution)/shard_map/pallas_call | solution.py:110
  79.8 3.5 %collective-permute-done.23 = bf16[128,2304]{1,0:T(8,128)(2,1)S(1)} collective-permute-done((bf16[128,2304]{1,0:T(8,128)(2,1)S(1)}, bf16[128,2304]{1,0:T(8,128)(2,1)S(1)}, u32[]{:S(2)}, u32[]{:S(2)}) %collective-permute-start.23) | collective-permute-done | bytes 589856 | tf_op jit(solution)/shard_map/ppermute | solution.py:47
  84.1 1.6 %collective-permute-done.25 = bf16[128,2304]{1,0:T(8,128)(2,1)S(1)} collective-permute-done((bf16[128,2304]{1,0:T(8,128)(2,1)S(1)}, bf16[128,2304]{1,0:T(8,128)(2,1)S(1)}, u32[]{:S(2)}, u32[]{:S(2)}) %collective-permute-start.25) | collective-permute-done | bytes 589856 | tf_op jit(solution)/shard_map/ppermute | solution.py:47
  87.5 3.1 %collective-permute-start.26 = (bf16[128,2304]{1,0:T(8,128)(2,1)S(1)}, bf16[128,2304]{1,0:T(8,128)(2,1)S(1)}, u32[]{:S(2)}, u32[]{:S(2)}) collective-permute-start(bf16[128,2304]{1,0:T(8,128)(2,1)S(1)} %slice.65), channel_id=1, source_target_pairs={{0,6},{1,7},{2,0},{3,1},{4,2},{5,3},{6,4},{7,5},{8,14},{9,15},{10,... | collective-permute-start | bytes 1769480 | tf_op jit(solution)/shard_map/ppermute | solution.py:47
  91.5 2.7 %copy-done = f32[2304,640]{1,0:T(8,128)S(1)} copy-done((f32[2304,640]{1,0:T(8,128)S(1)}, f32[2304,640]{1,0:T(8,128)}, u32[]{:S(2)}) %copy-start) | copy-done | bytes 5898264
  94.2 5.1 %shard_map.71 = bf16[2304,640]{1,0:T(8,128)(2,1)} custom-call(f32[2304,640]{1,0:T(8,128)S(1)} %copy-done, bf16[2304,640]{1,0:T(8,128)(2,1)S(1)} %collective-permute-done.29.got, bf16[2304,640]{1,0:T(8,128)(2,1)S(1)} %copy-done.1, bf16[2304,640]{1,0:T(8,128)(2,1)S(1)} %copy-done.2), custom_call_target="tpu_custom_call" | custom-call | bytes 17694720 | tf_op jit(solution)/shard_map/pallas_call | solution.py:134
  100.2 2.9 %collective-permute-done.27 = bf16[128,2304]{1,0:T(8,128)(2,1)S(1)} collective-permute-done((bf16[128,2304]{1,0:T(8,128)(2,1)S(1)}, bf16[128,2304]{1,0:T(8,128)(2,1)S(1)}, u32[]{:S(2)}, u32[]{:S(2)}) %collective-permute-start.27) | collective-permute-done | bytes 589856 | tf_op jit(solution)/shard_map/ppermute | solution.py:47
  (70 shorter events, 25.4 us)
Async XLA Ops:
  0.6 13.0 %collective-permute-start.3 = (bf16[2304,640]{1,0:T(8,128)(2,1)}, bf16[2304,640]{1,0:T(8,128)(2,1)}, u32[]{:S(2)}, u32[]{:S(2)}) collective-permute-start(bf16[2304,640]{1,0:T(8,128)(2,1)} %param.7), channel_id=1, source_target_pairs={{0,1},{1,0},{2,3},{3,2},{4,5},{5,4},{6,7},{7,6},{8,9},{9,8},{10,11... | collective-permute-start | bytes 8847368 | tf_op jit(solution)/shard_map/ppermute | solution.py:47
  0.7 8.8 %collective-permute-start = (bf16[128,640]{1,0:T(8,128)(2,1)}, bf16[128,640]{1,0:T(8,128)(2,1)S(1)}, u32[]{:S(2)}, u32[]{:S(2)}) collective-permute-start(bf16[128,640]{1,0:T(8,128)(2,1)} %param.6), channel_id=1, source_target_pairs={{0,128},{16,144},{32,160},{48,176},{64,192},{80,208},{96,224},{112... | collective-permute-start | bytes 491528 | tf_op jit(solution)/shard_map/ppermute | solution.py:52
  5.5 20.1 %collective-permute-start.10 = (bf16[2304,128]{1,0:T(8,128)(2,1)S(1)}, bf16[2304,128]{1,0:T(8,128)(2,1)S(1)}, u32[]{:S(2)}, u32[]{:S(2)}) collective-permute-start(bf16[2304,128]{1,0:T(8,128)(2,1)S(1)} %shard_map.68.refs_9_), channel_id=1, source_target_pairs={{0,8},{1,9},{2,10},{3,11},{4,12},{5,13},{6,14},{7,15},{8,0},{9,1},... | collective-permute-start | bytes 1769480 | tf_op jit(solution)/shard_map/ppermute | solution.py:47
  6.2 19.4 %collective-permute-start.11 = (bf16[2304,128]{1,0:T(8,128)(2,1)S(1)}, bf16[2304,128]{1,0:T(8,128)(2,1)S(1)}, u32[]{:S(2)}, u32[]{:S(2)}) collective-permute-start(bf16[2304,128]{1,0:T(8,128)(2,1)S(1)} %shard_map.68.refs_9_), channel_id=1, source_target_pairs={{0,2},{1,3},{2,4},{3,5},{4,6},{5,7},{6,0},{7,1},{8,10},{9,11},{10,... | collective-permute-start | bytes 1769480 | tf_op jit(solution)/shard_map/ppermute | solution.py:47
  7.8 19.2 %collective-permute-start.8 = (bf16[2304,128]{1,0:T(8,128)(2,1)S(1)}, bf16[2304,128]{1,0:T(8,128)(2,1)S(1)}, u32[]{:S(2)}, u32[]{:S(2)}) collective-permute-start(bf16[2304,128]{1,0:T(8,128)(2,1)S(1)} %shard_map.68.refs_9_), channel_id=1, source_target_pairs={{0,6},{1,7},{2,0},{3,1},{4,2},{5,3},{6,4},{7,5},{8,14},{9,15},{10,... | collective-permute-start | bytes 1769480 | tf_op jit(solution)/shard_map/ppermute | solution.py:47
  10.5 9.7 %collective-permute-start.1 = (bf16[2,128,640]{2,1,0:T(8,128)(2,1)S(1)}, bf16[2,128,640]{2,1,0:T(8,128)(2,1)S(1)}, u32[]{:S(2)}, u32[]{:S(2)}) collective-permute-start(bf16[2,128,640]{2,1,0:T(8,128)(2,1)S(1)} %pad_maximum_fusion.1.refs_0_), channel_id=1, source_target_pairs={{0,16},{16,32},{32,48},{48,64},{64,80},{80,96},{96,112},{112,0},{1... | collective-permute-start | bytes 983048 | tf_op jit(solution)/shard_map/ppermute | solution.py:52
  13.7 9.9 %collective-permute-start.2 = (bf16[2,128,640]{2,1,0:T(8,128)(2,1)S(1)}, bf16[2,128,640]{2,1,0:T(8,128)(2,1)S(1)}, u32[]{:S(2)}, u32[]{:S(2)}) collective-permute-start(bf16[2,128,640]{2,1,0:T(8,128)(2,1)S(1)} %pad_maximum_fusion.1.refs_0_), channel_id=1, source_target_pairs={{0,112},{16,0},{32,16},{48,32},{64,48},{80,64},{96,80},{112,96},{1... | collective-permute-start | bytes 983048 | tf_op jit(solution)/shard_map/ppermute | solution.py:52
  23.9 9.3 %collective-permute-start.4 = (bf16[2,128,640]{2,1,0:T(8,128)(2,1)S(1)}, bf16[2,128,640]{2,1,0:T(8,128)(2,1)S(1)}, u32[]{:S(2)}, u32[]{:S(2)}) collective-permute-start(bf16[2,128,640]{2,1,0:T(8,128)(2,1)S(1)} %collective-permute-done.2.refs_1_), channel_id=1, source_target_pairs={{0,112},{16,0},{32,16},{48,32},{64,48},{80,64},{96,80},{112,96},{1... | collective-permute-start | bytes 983048 | tf_op jit(solution)/shard_map/ppermute | solution.py:52
  25.6 14.2 %collective-permute-start.12 = (bf16[2304,128]{1,0:T(8,128)(2,1)S(1)}, bf16[2304,128]{1,0:T(8,128)(2,1)S(1)}, u32[]{:S(2)}, u32[]{:S(2)}) collective-permute-start(bf16[2304,128]{1,0:T(8,128)(2,1)S(1)} %collective-permute-done.10.refs_8_), channel_id=1, source_target_pairs={{0,2},{1,3},{2,4},{3,5},{4,6},{5,7},{6,0},{7,1},{8,10},{9,11},{10,... | collective-permute-start | bytes 1769480 | tf_op jit(solution)/shard_map/ppermute | solution.py:47
  27.0 12.8 %collective-permute-start.13 = (bf16[2304,128]{1,0:T(8,128)(2,1)S(1)}, bf16[2304,128]{1,0:T(8,128)(2,1)S(1)}, u32[]{:S(2)}, u32[]{:S(2)}) collective-permute-start(bf16[2304,128]{1,0:T(8,128)(2,1)S(1)} %collective-permute-done.8.refs_6_), channel_id=1, source_target_pairs={{0,8},{1,9},{2,10},{3,11},{4,12},{5,13},{6,14},{7,15},{8,0},{9,1},... | collective-permute-start | bytes 1769480 | tf_op jit(solution)/shard_map/ppermute | solution.py:47
  28.5 12.1 %collective-permute-start.9 = (bf16[2304,128]{1,0:T(8,128)(2,1)S(1)}, bf16[2304,128]{1,0:T(8,128)(2,1)S(1)}, u32[]{:S(2)}, u32[]{:S(2)}) collective-permute-start(bf16[2304,128]{1,0:T(8,128)(2,1)S(1)} %collective-permute-done.8.refs_6_), channel_id=1, source_target_pairs={{0,6},{1,7},{2,0},{3,1},{4,2},{5,3},{6,4},{7,5},{8,14},{9,15},{10,... | collective-permute-start | bytes 1769480 | tf_op jit(solution)/shard_map/ppermute | solution.py:47
  31.5 9.1 %collective-permute-start.6 = (bf16[2,128,640]{2,1,0:T(8,128)(2,1)S(1)}, bf16[2,128,640]{2,1,0:T(8,128)(2,1)S(1)}, u32[]{:S(2)}, u32[]{:S(2)}) collective-permute-start(bf16[2,128,640]{2,1,0:T(8,128)(2,1)S(1)} %collective-permute-done.5.refs_5_), channel_id=1, source_target_pairs={{0,16},{16,32},{32,48},{48,64},{64,80},{80,96},{96,112},{112,0},{1... | collective-permute-start | bytes 983048 | tf_op jit(solution)/shard_map/ppermute | solution.py:52
  33.1 8.3 %collective-permute-start.7 = (bf16[2,128,640]{2,1,0:T(8,128)(2,1)S(1)}, bf16[2,128,640]{2,1,0:T(8,128)(2,1)S(1)}, u32[]{:S(2)}, u32[]{:S(2)}) collective-permute-start(bf16[2,128,640]{2,1,0:T(8,128)(2,1)S(1)} %collective-permute-done.4.refs_2_), channel_id=1, source_target_pairs={{0,112},{16,0},{32,16},{48,32},{64,48},{80,64},{96,80},{112,96},{1... | collective-permute-start | bytes 983048 | tf_op jit(solution)/shard_map/ppermute | solution.py:52
  50.4 11.2 %collective-permute-start.20 = (bf16[768,128]{1,0:T(8,128)(2,1)S(1)}, bf16[768,128]{1,0:T(8,128)(2,1)S(1)}, u32[]{:S(2)}, u32[]{:S(2)}) collective-permute-start(bf16[768,128]{1,0:T(8,128)(2,1)S(1)} %slice.58), channel_id=1, source_target_pairs={{0,6},{1,7},{2,0},{3,1},{4,2},{5,3},{6,4},{7,5},{8,14},{9,15},{10,... | collective-permute-start | bytes 589832 | tf_op jit(solution)/shard_map/ppermute | solution.py:47
  53.6 14.7 %collective-permute-start.21 = (bf16[768,128]{1,0:T(8,128)(2,1)S(1)}, bf16[768,128]{1,0:T(8,128)(2,1)S(1)}, u32[]{:S(2)}, u32[]{:S(2)}) collective-permute-start(bf16[768,128]{1,0:T(8,128)(2,1)S(1)} %slice.59), channel_id=1, source_target_pairs={{0,2},{1,3},{2,4},{3,5},{4,6},{5,7},{6,0},{7,1},{8,10},{9,11},{10,... | collective-permute-start | bytes 589832 | tf_op jit(solution)/shard_map/ppermute | solution.py:47
  53.7 14.6 %collective-permute-start.22 = (bf16[768,128]{1,0:T(8,128)(2,1)S(1)}, bf16[768,128]{1,0:T(8,128)(2,1)S(1)}, u32[]{:S(2)}, u32[]{:S(2)}) collective-permute-start(bf16[768,128]{1,0:T(8,128)(2,1)S(1)} %slice.60), channel_id=1, source_target_pairs={{0,8},{1,9},{2,10},{3,11},{4,12},{5,13},{6,14},{7,15},{8,0},{9,1},... | collective-permute-start | bytes 589832 | tf_op jit(solution)/shard_map/ppermute | solution.py:47
  58.3 10.0 %collective-permute-start.17 = (bf16[128,768]{1,0:T(8,128)(2,1)S(1)}, bf16[128,768]{1,0:T(8,128)(2,1)S(1)}, u32[]{:S(2)}, u32[]{:S(2)}) collective-permute-start(bf16[128,768]{1,0:T(8,128)(2,1)S(1)} %get-tuple-element.105), channel_id=1, source_target_pairs={{0,2},{1,3},{2,4},{3,5},{4,6},{5,7},{6,0},{7,1},{8,10},{9,11},{10,... | collective-permute-start | bytes 589832 | tf_op jit(solution)/shard_map/ppermute | solution.py:47
  58.4 9.9 %collective-permute-start.18 = (bf16[128,768]{1,0:T(8,128)(2,1)S(1)}, bf16[128,768]{1,0:T(8,128)(2,1)S(1)}, u32[]{:S(2)}, u32[]{:S(2)}) collective-permute-start(bf16[128,768]{1,0:T(8,128)(2,1)S(1)} %get-tuple-element.104), channel_id=1, source_target_pairs={{0,6},{1,7},{2,0},{3,1},{4,2},{5,3},{6,4},{7,5},{8,14},{9,15},{10,... | collective-permute-start | bytes 589832 | tf_op jit(solution)/shard_map/ppermute | solution.py:47
  68.5 14.7 %collective-permute-start.23 = (bf16[128,2304]{1,0:T(8,128)(2,1)S(1)}, bf16[128,2304]{1,0:T(8,128)(2,1)S(1)}, u32[]{:S(2)}, u32[]{:S(2)}) collective-permute-start(bf16[128,2304]{1,0:T(8,128)(2,1)S(1)} %get-tuple-element.102), channel_id=1, source_target_pairs={{0,8},{1,9},{2,10},{3,11},{4,12},{5,13},{6,14},{7,15},{8,0},{9,1},... | collective-permute-start | bytes 1769480 | tf_op jit(solution)/shard_map/ppermute | solution.py:47
  69.8 14.3 %collective-permute-start.24 = (bf16[128,2304]{1,0:T(8,128)(2,1)S(1)}, bf16[128,2304]{1,0:T(8,128)(2,1)S(1)}, u32[]{:S(2)}, u32[]{:S(2)}) collective-permute-start(bf16[128,2304]{1,0:T(8,128)(2,1)S(1)} %get-tuple-element.101), channel_id=1, source_target_pairs={{0,6},{1,7},{2,0},{3,1},{4,2},{5,3},{6,4},{7,5},{8,14},{9,15},{10,... | collective-permute-start | bytes 1769480 | tf_op jit(solution)/shard_map/ppermute | solution.py:47
  70.8 14.9 %collective-permute-start.25 = (bf16[128,2304]{1,0:T(8,128)(2,1)S(1)}, bf16[128,2304]{1,0:T(8,128)(2,1)S(1)}, u32[]{:S(2)}, u32[]{:S(2)}) collective-permute-start(bf16[128,2304]{1,0:T(8,128)(2,1)S(1)} %get-tuple-element.100), channel_id=1, source_target_pairs={{0,2},{1,3},{2,4},{3,5},{4,6},{5,7},{6,0},{7,1},{8,10},{9,11},{10,... | collective-permute-start | bytes 1769480 | tf_op jit(solution)/shard_map/ppermute | solution.py:47
  86.2 17.0 %collective-permute-start.27 = (bf16[128,2304]{1,0:T(8,128)(2,1)S(1)}, bf16[128,2304]{1,0:T(8,128)(2,1)S(1)}, u32[]{:S(2)}, u32[]{:S(2)}) collective-permute-start(bf16[128,2304]{1,0:T(8,128)(2,1)S(1)} %get-tuple-element.88), channel_id=1, source_target_pairs={{0,2},{1,3},{2,4},{3,5},{4,6},{5,7},{6,0},{7,1},{8,10},{9,11},{10,... | collective-permute-start | bytes 1769480 | tf_op jit(solution)/shard_map/ppermute | solution.py:47
  86.4 16.8 %collective-permute-start.28 = (bf16[128,2304]{1,0:T(8,128)(2,1)S(1)}, bf16[128,2304]{1,0:T(8,128)(2,1)S(1)}, u32[]{:S(2)}, u32[]{:S(2)}) collective-permute-start(bf16[128,2304]{1,0:T(8,128)(2,1)S(1)} %get-tuple-element.89), channel_id=1, source_target_pairs={{0,8},{1,9},{2,10},{3,11},{4,12},{5,13},{6,14},{7,15},{8,0},{9,1},... | collective-permute-start | bytes 1769480 | tf_op jit(solution)/shard_map/ppermute | solution.py:47
  87.5 15.8 %collective-permute-start.26 = (bf16[128,2304]{1,0:T(8,128)(2,1)S(1)}, bf16[128,2304]{1,0:T(8,128)(2,1)S(1)}, u32[]{:S(2)}, u32[]{:S(2)}) collective-permute-start(bf16[128,2304]{1,0:T(8,128)(2,1)S(1)} %slice.65), channel_id=1, source_target_pairs={{0,6},{1,7},{2,0},{3,1},{4,2},{5,3},{6,4},{7,5},{8,14},{9,15},{10,... | collective-permute-start | bytes 1769480 | tf_op jit(solution)/shard_map/ppermute | solution.py:47
  (12 other events, 88.3 us)
